TPU v7x, 128 devices: a whole 4x4x4 slice. The times are simulated.
128 devices in a mesh: fs: 16 (over z, x), sp: 8 (over y, core).
Axes of the slice: x: 4, y: 4, z: 4, core: 2. Of those that a mesh axis runs over, the one named last changes fastest.
Arguments:
- layer_input: bfloat16 [16, 1024, 2048], P('fs', 'sp'), may hold values from -6 to 6
- output_gradient: bfloat16 [16, 1024, 2048], P('fs', 'sp'), may hold values from -6 to 6
- norm_gain_pair: float32 [2, 2048], replicated, may hold values from 0.25 to 1.75
- query_key_value_weight: bfloat16 [2048, 3, 2048], P('fs'), may hold values from -0.125 to 0.125
- output_weight: bfloat16 [2048, 2048], P('fs'), may hold values from -0.25 to 0.25
- gate_up_weight: bfloat16 [2048, 2, 8192], P('fs'), may hold values from -0.125 to 0.125
- down_weight: bfloat16 [8192, 2048], P('fs'), may hold values from -0.0625 to 0.0625
- adapter_input_model: bfloat16 [6, 2048, 128], P(None, 'fs'), may hold values from -0.125 to 0.125
- adapter_output_model: bfloat16 [5, 2048, 128], P(None, 'fs'), may hold values from -0.75 to 0.75
- adapter_input_hidden: bfloat16 [1, 8192, 128], P(None, 'fs'), may hold values from -0.0625 to 0.0625
- adapter_output_hidden: bfloat16 [2, 8192, 128], P(None, 'fs'), may hold values from -0.75 to 0.75
- spans: int32 [16, 3], P('fs'), may hold values from 1 to 512, 1024 in all within a row
- adapter_choice_rows: int32 [16, 3], P('fs'), may hold values from 0 to 7
Outputs:
- layer_output: bfloat16 [16, 1024, 2048], P('fs', 'sp')
- grad_in: float32 [16, 1024, 2048], P('fs', 'sp')
- grad_lora_in_d: float32 [6, 2048, 128], P(None, 'fs')
- grad_lora_out_d: float32 [5, 2048, 128], P(None, 'fs')
- grad_lora_in_ff: float32 [1, 8192, 128], P(None, 'fs')
- grad_lora_out_ff: float32 [2, 8192, 128], P(None, 'fs')
Inputs may be any that keep to these rules, and one draw needn't show every extreme that they name: `spans`: per group, the prompt, first continuation and second continuation lie end to end in that order and fill all 1024 tokens; the longest is 512.
All inputs are finite; a program needn't handle non-finite values.
Results may differ from a plain program's by a relative error of at most 0.02.
Values may be sent and summed in bfloat16 or wider, within the bound.
No kernel may reach another device: no remote copies, remote signals or barrier semaphores. Data moves between devices by JAX's collectives and lax.ppermute only.
A program may use at most 512 MiB of HBM per device.

v0:
```python
import jax
import jax.numpy as jnp
from jax import lax
from jax.sharding import PartitionSpec as P

HEAD_SIZE = 64
ADAPTER_RANK = 16


NORM_EPS = 1e-05
ROPE_BASE = 130000.0
MASK_FILL = -1e30


def for_sending(x):
    return jax.tree.map(lambda a: a.astype(jnp.bfloat16) if a.dtype == jnp.float32 else a, x)


def over_all_2(x, axis, dim, block):
    whole = lax.all_gather(x, axis, axis=dim, tiled=True)
    return block(whole, jnp.int32(0))


def matrix_product(left, right):
    return jnp.dot(left, right, preferred_element_type=jnp.float32)


def matrix_product_transposed(left, right):
    return lax.dot_general(
        left, right, (((1,), (1,)), ((), ())), preferred_element_type=jnp.float32
    )


def matmul_tn(left, right):
    return lax.dot_general(
        left, right, (((0,), (0,)), ((), ())), preferred_element_type=jnp.float32
    )


def angles(position):
    half_dim = HEAD_SIZE // 2
    freq = ROPE_BASE ** (-(jnp.arange(half_dim, dtype=jnp.float32) * 2.0 / HEAD_SIZE))
    phase = position.astype(jnp.float32)[:, None] * freq[None, :]
    return (jnp.cos(phase)[:, None, :], jnp.sin(phase)[:, None, :])


def rotate(values, cosine, sine_part):
    half_dim = values.shape[-1] // 2
    first_half = values[..., :half_dim]
    second_half = values[..., half_dim:]
    return jnp.concatenate(
        [
            first_half * cosine - second_half * sine_part,
            second_half * cosine + first_half * sine_part,
        ],
        -1,
    )


def token_info(spans, adapter_choice_rows, group_tokens):
    token_pos = jnp.arange(group_tokens, dtype=jnp.int32)[None, :]
    prompt_len = spans[..., 0:1]
    first_len = spans[..., 1:2]
    segment = (token_pos >= prompt_len).astype(jnp.int32) + (
        token_pos >= prompt_len + first_len
    ).astype(jnp.int32)
    position = token_pos - jnp.where(segment == 2, first_len, 0)
    chosen = jnp.where(
        segment == 0,
        adapter_choice_rows[..., 0:1],
        jnp.where(segment == 1, adapter_choice_rows[..., 1:2], adapter_choice_rows[..., 2:3]),
    )
    return (segment, position, chosen)


def allowed_mask(segment, offset, block_rows):
    key_idx = jnp.arange(segment.shape[0])
    query_idx = offset + jnp.arange(block_rows)
    query_seg = segment[offset : offset + block_rows]
    return (key_idx[None, :] <= query_idx[:, None]) & (
        (segment[None, :] == query_seg[:, None]) | (segment[None, :] == 0)
    )


def norm_back(grad_norm, values, inverse, gain):
    normed = values * inverse
    scaled = grad_norm * gain
    return inverse * (scaled - normed * jnp.mean(scaled * normed, -1, keepdims=True))


def reduced_rank_forward(source, down_map, up_map, adapter_select_mask):
    low_rank = (matrix_product(source, down_map) * adapter_select_mask).astype(jnp.bfloat16)
    return (matrix_product_transposed(low_rank, up_map), low_rank)


def reduced_rank_backward(gradient_row_block, down_map, up_map, masked_reduced):
    grad_low = matrix_product(gradient_row_block, up_map).astype(jnp.bfloat16) * masked_reduced
    return (matrix_product_transposed(grad_low, down_map), grad_low)


def attend(query_all, key_all, value_all, segment):
    group_tokens = query_all.shape[0]
    head_split = query_all.shape[1] // HEAD_SIZE
    key_heads = key_all.reshape(group_tokens, head_split, HEAD_SIZE)
    value_heads = value_all.reshape(group_tokens, head_split, HEAD_SIZE)
    block_rows = min(512, group_tokens)
    scale = HEAD_SIZE ** (-0.5)
    outputs = []
    log_parts = []
    for offset in range(0, group_tokens, block_rows):
        query_block = query_all[offset : offset + block_rows].reshape(
            block_rows, head_split, HEAD_SIZE
        )
        scores = (
            jnp.einsum("qhd,khd->hqk", query_block, key_heads, preferred_element_type=jnp.float32)
            * scale
        )
        scores = jnp.where(allowed_mask(segment, offset, block_rows)[None], scores, MASK_FILL)
        row_max = jnp.max(scores, -1, keepdims=True)
        exp_scores = jnp.exp(scores - row_max)
        row_total = jnp.sum(exp_scores, -1, keepdims=True)
        softmax_w = (exp_scores / row_total).astype(jnp.bfloat16)
        block_out = jnp.einsum(
            "hqk,khd->qhd", softmax_w, value_heads, preferred_element_type=jnp.float32
        )
        outputs.append(block_out.astype(jnp.bfloat16).reshape(block_rows, head_split * HEAD_SIZE))
        log_parts.append((row_max + jnp.log(row_total))[..., 0])
    return (jnp.concatenate(outputs, 0), jnp.concatenate(log_parts, 1))


def attend_back(query_all, key_all, value_all, grad_all, log_total, segment):
    group_tokens = query_all.shape[0]
    head_split = query_all.shape[1] // HEAD_SIZE
    key_heads = key_all.reshape(group_tokens, head_split, HEAD_SIZE)
    value_heads = value_all.reshape(group_tokens, head_split, HEAD_SIZE)
    block_rows = min(512, group_tokens)
    scale = HEAD_SIZE ** (-0.5)
    key_grad = jnp.zeros((group_tokens, head_split, HEAD_SIZE), jnp.float32)
    value_grad = jnp.zeros((group_tokens, head_split, HEAD_SIZE), jnp.float32)
    query_grads = []
    for offset in range(0, group_tokens, block_rows):
        query_block = query_all[offset : offset + block_rows].reshape(
            block_rows, head_split, HEAD_SIZE
        )
        grad_block = grad_all[offset : offset + block_rows].reshape(
            block_rows, head_split, HEAD_SIZE
        )
        scores = (
            jnp.einsum("qhd,khd->hqk", query_block, key_heads, preferred_element_type=jnp.float32)
            * scale
        )
        scores = jnp.where(allowed_mask(segment, offset, block_rows)[None], scores, MASK_FILL)
        softmax_f = jnp.exp(scores - log_total[:, offset : offset + block_rows, None])
        grad_w = jnp.einsum(
            "qhd,khd->hqk", grad_block, value_heads, preferred_element_type=jnp.float32
        )
        inner_sum = jnp.sum(softmax_f * grad_w, -1, keepdims=True)
        grad_scores = (softmax_f * (grad_w - inner_sum)).astype(jnp.bfloat16)
        query_grad = (
            jnp.einsum("hqk,khd->qhd", grad_scores, key_heads, preferred_element_type=jnp.float32)
            * scale
        )
        query_grads.append(
            query_grad.astype(jnp.bfloat16).reshape(block_rows, head_split * HEAD_SIZE)
        )
        key_grad = (
            key_grad
            + jnp.einsum(
                "hqk,qhd->khd", grad_scores, query_block, preferred_element_type=jnp.float32
            )
            * scale
        )
        value_grad = value_grad + jnp.einsum(
            "hqk,qhd->khd",
            softmax_f.astype(jnp.bfloat16),
            grad_block,
            preferred_element_type=jnp.float32,
        )
    key_out = key_grad.astype(jnp.bfloat16).reshape(group_tokens, head_split * HEAD_SIZE)
    value_out = value_grad.astype(jnp.bfloat16).reshape(group_tokens, head_split * HEAD_SIZE)
    return (jnp.concatenate(query_grads, 0), key_out, value_out)


def body(
    layer_input,
    output_gradient,
    norm_gain_pair,
    query_key_value_weight,
    output_weight,
    gate_up_weight,
    down_weight,
    adapter_input_model,
    adapter_output_model,
    adapter_input_hidden,
    adapter_output_hidden,
    spans,
    adapter_choice_rows,
):
    groups, local_rows, width_of_model = layer_input.shape
    count_of_rows = groups * local_rows
    group_tokens = local_rows * lax.axis_size("sp")
    token_start = lax.axis_index("sp") * local_rows
    head_split = width_of_model // HEAD_SIZE
    token_shaped = (groups, local_rows, width_of_model)
    input_model_map, output_model_map, input_hidden_map, output_hidden_map = (
        lax.all_gather(adapter_input_model, "fs", axis=1, tiled=True),
        lax.all_gather(adapter_output_model, "fs", axis=1, tiled=True),
        lax.all_gather(adapter_input_hidden, "fs", axis=1, tiled=True),
        lax.all_gather(adapter_output_hidden, "fs", axis=1, tiled=True),
    )
    hidden_feedforward = input_hidden_map.shape[1]
    rank_cols = input_model_map.shape[2]
    wqkv, output_matrix = (
        lax.all_gather(query_key_value_weight, "fs", axis=0, tiled=True),
        lax.all_gather(output_weight, "fs", axis=0, tiled=True),
    )
    wqkv_flat = wqkv.reshape(width_of_model, 3 * width_of_model)
    segment, position, chosen = token_info(spans, adapter_choice_rows, group_tokens)
    local_pos = lax.dynamic_slice_in_dim(position, token_start, local_rows, 1).reshape(
        count_of_rows
    )
    local_choice = lax.dynamic_slice_in_dim(chosen, token_start, local_rows, 1).reshape(
        count_of_rows
    )
    adapter_select_mask = (
        local_choice[:, None] == jnp.arange(rank_cols)[None, :] // ADAPTER_RANK
    ).astype(jnp.float32)
    masked_reduced = adapter_select_mask.astype(jnp.bfloat16)
    cosine, sine_part = angles(local_pos)
    gain_attn = norm_gain_pair[0]
    gain_mlp = norm_gain_pair[1]
    input_single_float = layer_input.astype(jnp.float32).reshape(count_of_rows, width_of_model)
    inv_attn = lax.rsqrt(
        jnp.mean(input_single_float * input_single_float, -1, keepdims=True) + NORM_EPS
    )
    normalized_first = (input_single_float * inv_attn * gain_attn).astype(jnp.bfloat16)
    query_key_value_base = matrix_product(normalized_first, wqkv_flat)
    adapter_query_term, reduced_query = reduced_rank_forward(
        normalized_first, input_model_map[0], output_model_map[0], adapter_select_mask
    )
    adapter_key_term, reduced_key = reduced_rank_forward(
        normalized_first, input_model_map[1], output_model_map[1], adapter_select_mask
    )
    adapter_value_term, reduced_value = reduced_rank_forward(
        normalized_first, input_model_map[2], output_model_map[2], adapter_select_mask
    )
    query_preact = (query_key_value_base[:, :width_of_model] + adapter_query_term).reshape(
        count_of_rows, head_split, HEAD_SIZE
    )
    key_preact = (
        query_key_value_base[:, width_of_model : 2 * width_of_model] + adapter_key_term
    ).reshape(count_of_rows, head_split, HEAD_SIZE)
    query_tok = rotate(query_preact, cosine, sine_part).astype(jnp.bfloat16).reshape(token_shaped)
    key_tok = rotate(key_preact, cosine, sine_part).astype(jnp.bfloat16).reshape(token_shaped)
    value_tokens = (
        (query_key_value_base[:, 2 * width_of_model :] + adapter_value_term)
        .astype(jnp.bfloat16)
        .reshape(token_shaped)
    )
    query_heads, key_heads, value_heads = (
        lax.all_to_all(query_tok, "sp", split_axis=2, concat_axis=1, tiled=True),
        lax.all_to_all(key_tok, "sp", split_axis=2, concat_axis=1, tiled=True),
        lax.all_to_all(value_tokens, "sp", split_axis=2, concat_axis=1, tiled=True),
    )
    mix_heads, log_total = lax.map(
        lambda group_item: attend(*group_item), (query_heads, key_heads, value_heads, segment)
    )
    attention_mixed = jax.tree.map(
        lambda part, own: part.astype(own.dtype),
        lax.all_to_all(for_sending(mix_heads), "sp", split_axis=1, concat_axis=2, tiled=True),
        mix_heads,
    ).reshape(count_of_rows, width_of_model)
    adapter_output_term, reduced_output = reduced_rank_forward(
        attention_mixed, input_model_map[3], output_model_map[3], adapter_select_mask
    )
    residual_stream = (
        input_single_float + matrix_product(attention_mixed, output_matrix) + adapter_output_term
    )
    inv_mlp = lax.rsqrt(jnp.mean(residual_stream * residual_stream, -1, keepdims=True) + NORM_EPS)
    normalized_second = (residual_stream * inv_mlp * gain_mlp).astype(jnp.bfloat16)
    add_weight_piece = lax.all_gather(gate_up_weight, "fs", axis=0, tiled=True)
    piece_rows = add_weight_piece.shape[0]
    columns = lax.slice_in_dim(normalized_second, 0, piece_rows, axis=1)
    gate_up_pair = jnp.zeros((count_of_rows, 2 * hidden_feedforward), jnp.float32) + matrix_product(
        columns, add_weight_piece.reshape(piece_rows, 2 * hidden_feedforward)
    )
    adapter_gate_term, reduced_gate = reduced_rank_forward(
        normalized_second, input_model_map[4], output_hidden_map[0], adapter_select_mask
    )
    adapter_up_term, reduced_up = reduced_rank_forward(
        normalized_second, input_model_map[5], output_hidden_map[1], adapter_select_mask
    )
    gate_preact = gate_up_pair[:, :hidden_feedforward] + adapter_gate_term
    up_preact = gate_up_pair[:, hidden_feedforward:] + adapter_up_term
    gate_sig = jax.nn.sigmoid(gate_preact)
    gate_act = gate_preact * gate_sig
    hidden_activated = (gate_act * up_preact).astype(jnp.bfloat16)

    def add_down(running, weight_piece):
        columns = lax.slice_in_dim(hidden_activated, 0, weight_piece.shape[0], axis=1)
        return running + matrix_product(columns, weight_piece)

    down_portion = add_down(
        jnp.zeros((count_of_rows, width_of_model), jnp.float32),
        lax.all_gather(down_weight, "fs", axis=0, tiled=True),
    )
    adapter_down_term, reduced_down = reduced_rank_forward(
        hidden_activated, input_hidden_map[0], output_model_map[4], adapter_select_mask
    )
    layer_output = (
        (residual_stream + down_portion + adapter_down_term)
        .astype(jnp.bfloat16)
        .reshape(token_shaped)
    )
    gradient_row_block = output_gradient.reshape(count_of_rows, width_of_model)
    hidden_adapter_term, gradient_low_down = reduced_rank_backward(
        gradient_row_block, input_hidden_map[0], output_model_map[4], masked_reduced
    )
    gradient_hidden_units = over_all_2(
        down_weight,
        "fs",
        0,
        lambda weight_piece, offset: matrix_product_transposed(gradient_row_block, weight_piece),
    )
    gradient_hidden_units = gradient_hidden_units + hidden_adapter_term
    grad_gate = (
        gradient_hidden_units * up_preact * gate_sig * (1.0 + gate_preact * (1.0 - gate_sig))
    ).astype(jnp.bfloat16)
    grad_up = (gradient_hidden_units * gate_act).astype(jnp.bfloat16)
    grad_gate_up = jnp.concatenate([grad_gate, grad_up], 1)
    grad_normed_two = over_all_2(
        gate_up_weight,
        "fs",
        0,
        lambda weight_piece, offset: matrix_product_transposed(
            grad_gate_up, weight_piece.reshape(weight_piece.shape[0], 2 * hidden_feedforward)
        ),
    )
    norm_g, glow_g = reduced_rank_backward(
        grad_gate, input_model_map[4], output_hidden_map[0], masked_reduced
    )
    norm_u, glow_u = reduced_rank_backward(
        grad_up, input_model_map[5], output_hidden_map[1], masked_reduced
    )
    grad_resid = gradient_row_block.astype(jnp.float32) + norm_back(
        grad_normed_two + norm_g + norm_u, residual_stream, inv_mlp, gain_mlp
    )
    gradient_attention = grad_resid.astype(jnp.bfloat16)
    mixed_adapter_term, gradient_low_output = reduced_rank_backward(
        gradient_attention, input_model_map[3], output_model_map[3], masked_reduced
    )
    gradient_mixed = (
        (matrix_product_transposed(gradient_attention, output_matrix) + mixed_adapter_term)
        .astype(jnp.bfloat16)
        .reshape(token_shaped)
    )
    grad_mix_heads = lax.all_to_all(gradient_mixed, "sp", split_axis=2, concat_axis=1, tiled=True)
    grad_q_heads, grad_k_heads, grad_v_heads = lax.map(
        lambda group_item: attend_back(*group_item),
        (query_heads, key_heads, value_heads, grad_mix_heads, log_total, segment),
    )
    grad_q_tok, grad_k_tok, grad_v_tok = (
        lax.all_to_all(
            for_sending(grad_q_heads), "sp", split_axis=1, concat_axis=2, tiled=True
        ).astype(grad_q_heads.dtype),
        lax.all_to_all(
            for_sending(grad_k_heads), "sp", split_axis=1, concat_axis=2, tiled=True
        ).astype(grad_k_heads.dtype),
        lax.all_to_all(
            for_sending(grad_v_heads), "sp", split_axis=1, concat_axis=2, tiled=True
        ).astype(grad_v_heads.dtype),
    )
    grad_query = (
        rotate(
            grad_q_tok.astype(jnp.float32).reshape(count_of_rows, head_split, HEAD_SIZE),
            cosine,
            -sine_part,
        )
        .reshape(count_of_rows, width_of_model)
        .astype(jnp.bfloat16)
    )
    grad_key = (
        rotate(
            grad_k_tok.astype(jnp.float32).reshape(count_of_rows, head_split, HEAD_SIZE),
            cosine,
            -sine_part,
        )
        .reshape(count_of_rows, width_of_model)
        .astype(jnp.bfloat16)
    )
    grad_value = grad_v_tok.reshape(count_of_rows, width_of_model)
    grad_normed_one = matrix_product_transposed(
        jnp.concatenate([grad_query, grad_key, grad_value], 1), wqkv_flat
    )
    norm_q, glow_q = reduced_rank_backward(
        grad_query, input_model_map[0], output_model_map[0], masked_reduced
    )
    norm_k, glow_k = reduced_rank_backward(
        grad_key, input_model_map[1], output_model_map[1], masked_reduced
    )
    norm_v, glow_v = reduced_rank_backward(
        grad_value, input_model_map[2], output_model_map[2], masked_reduced
    )
    grad_normed_one = grad_normed_one + norm_q + norm_k + norm_v
    grad_in = (
        grad_resid + norm_back(grad_normed_one, input_single_float, inv_attn, gain_attn)
    ).reshape(token_shaped)
    local_in_d = jnp.stack(
        [
            matmul_tn(normalized_first, glow_q),
            matmul_tn(normalized_first, glow_k),
            matmul_tn(normalized_first, glow_v),
            matmul_tn(attention_mixed, gradient_low_output),
            matmul_tn(normalized_second, glow_g),
            matmul_tn(normalized_second, glow_u),
        ]
    )
    local_out_d = jnp.stack(
        [
            matmul_tn(grad_query, reduced_query),
            matmul_tn(grad_key, reduced_key),
            matmul_tn(grad_value, reduced_value),
            matmul_tn(gradient_attention, reduced_output),
            matmul_tn(gradient_row_block, reduced_down),
        ]
    )
    local_in_ff = matmul_tn(hidden_activated, gradient_low_down)[None]
    local_out_ff = jnp.stack([matmul_tn(grad_gate, reduced_gate), matmul_tn(grad_up, reduced_up)])
    shard_sums = (
        lax.psum_scatter(
            local_in_d.astype(jnp.bfloat16), "fs", scatter_dimension=1, tiled=True
        ).astype(jnp.float32),
        lax.psum_scatter(
            local_out_d.astype(jnp.bfloat16), "fs", scatter_dimension=1, tiled=True
        ).astype(jnp.float32),
        lax.psum_scatter(
            local_in_ff.astype(jnp.bfloat16), "fs", scatter_dimension=1, tiled=True
        ).astype(jnp.float32),
        lax.psum_scatter(
            local_out_ff.astype(jnp.bfloat16), "fs", scatter_dimension=1, tiled=True
        ).astype(jnp.float32),
    )
    sum_in_d, sum_out_d, sum_in_ff, sum_out_ff = (
        lax.psum(shard_sums[0].astype(jnp.bfloat16), "sp").astype(jnp.float32),
        lax.psum(shard_sums[1].astype(jnp.bfloat16), "sp").astype(jnp.float32),
        lax.psum(shard_sums[2].astype(jnp.bfloat16), "sp").astype(jnp.float32),
        lax.psum(shard_sums[3].astype(jnp.bfloat16), "sp").astype(jnp.float32),
    )
    return (layer_output, grad_in, sum_in_d, sum_out_d, sum_in_ff, sum_out_ff)


def solution(mesh):
    in_specs = (
        P("fs", "sp", None),
        P("fs", "sp", None),
        P(),
        P("fs", None, None),
        P("fs", None),
        P("fs", None, None),
        P("fs", None),
        P(None, "fs", None),
        P(None, "fs", None),
        P(None, "fs", None),
        P(None, "fs", None),
        P("fs", None),
        P("fs", None),
    )
    out_specs = (
        P("fs", "sp", None),
        P("fs", "sp", None),
        P(None, "fs", None),
        P(None, "fs", None),
        P(None, "fs", None),
        P(None, "fs", None),
    )
    return jax.shard_map(body, mesh=mesh, in_specs=in_specs, out_specs=out_specs, check_vma=False)
```

profile of v0, /device:TPU:0, one launch (start us, length us, event | category | flops | bytes accessed | tf_op | source)
XLA Modules:
  0.0 1591.8 jit_solution(10255654160929463409)
XLA Ops:
  20.6 40.1 %all-gather.11.cloned.1.call-done = bf16[6,2048,128]{2,1,0:T(8,128)(2,1)} async-done(((bf16[6,128,128]{2,1,0:T(8,128)(2,1)}), bf16[6,2048,128]{2,1,0:T(8,128)(2,1)}) %all-gather.11.cloned.1.call-update) | async-done | bytes 3145744 | tf_op jit(solution)/shard_map/all_gather | solution.py:206
  65.0 160.6 %all-gather.9.cloned.1.call-done = bf16[2048,3,2048]{0,2,1:T(8,128)(2,1)} async-done(((bf16[128,3,2048]{0,2,1:T(8,128)(2,1)}), bf16[2048,3,2048]{0,2,1:T(8,128)(2,1)}) %all-gather.9.cloned.1.call-update) | async-done | bytes 25165840 | tf_op jit(solution)/shard_map/all_gather | solution.py:214
  225.6 14.7 fusion.134
  240.3 33.1 %all-gather.13.cloned.1.call-done = bf16[5,2048,128]{2,1,0:T(8,128)(2,1)} async-done(((bf16[5,128,128]{2,1,0:T(8,128)(2,1)}), bf16[5,2048,128]{2,1,0:T(8,128)(2,1)}) %all-gather.13.cloned.1.call-update) | async-done | bytes 2621456 | tf_op jit(solution)/shard_map/all_gather | solution.py:207
  276.4 11.4 reduce
  300.0 8.1 copy.123
  308.1 11.5 reduce.2
  326.4 8.1 copy.124
  334.6 11.4 reduce.1
  392.6 8.2 all-to-all-done.3
  414.2 130.2 %all-gather.21.cloned.1.call-done = bf16[8192,2048]{1,0:T(8,128)(2,1)} async-done(((bf16[512,2048]{1,0:T(8,128)(2,1)}), bf16[8192,2048]{1,0:T(8,128)(2,1)}) %all-gather.21.cloned.1.call-update) | async-done | bytes 33554448 | tf_op jit(solution)/shard_map/all_gather | solution.py:305
  544.4 17.5 %fusion.113 = f32[128,8192]{1,0:T(8,128)} fusion(bf16[8192,2048]{1,0:T(8,128)(2,1)} %all-gather.21.cloned.1.call-done, bf16[1,128,2048]{2,1,0:T(8,128)(2,1)S(1)} %copy-done.14), kind=kOutput, calls=%fused_computation.193 | convolution fusion | flops 4294967296 | bytes 38273024 | tf_op jit(solution)/shard_map/dot_general | solution.py:29
  561.9 29.4 %all-gather.23.cloned.1.call-done = bf16[1,8192,128]{2,1,0:T(8,128)(2,1)} async-done(((bf16[1,512,128]{2,1,0:T(8,128)(2,1)}), bf16[1,8192,128]{2,1,0:T(8,128)(2,1)}) %all-gather.23.cloned.1.call-update) | async-done | bytes 2097168 | tf_op jit(solution)/shard_map/all_gather | solution.py:208
  596.9 364.6 %all-gather.17.cloned.1.call-done = bf16[2048,2,8192]{2,1,0:T(2,128)(2,1)} async-done(((bf16[128,2,8192]{2,1,0:T(2,128)(2,1)}), bf16[2048,2,8192]{2,1,0:T(2,128)(2,1)}) %all-gather.17.cloned.1.call-update) | async-done | bytes 67108880 | tf_op jit(solution)/shard_map/all_gather | solution.py:281
  961.5 55.6 %copy.116 = bf16[256,8,2,8192]{3,1,2,0:T(8,128)(2,1)} copy(bf16[256,8,2,8192]{3,2,1,0:T(2,128)(2,1)} %bitcast.110) | data formatting | bytes 134217728
  1017.1 26.3 %fusion.144 = f32[128,16384]{1,0:T(8,128)} fusion(bf16[128,2048]{1,0:T(8,128)(2,1)S(1)} %multiply_convert_fusion.5, bf16[2048,16384]{1,0:T(8,128)(2,1)} %bitcast.111), kind=kOutput, calls=%fused_computation.254 | convolution fusion | flops 8589934592 | bytes 76021760 | tf_op jit(solution)/shard_map/dot_general | solution.py:25
  1048.6 6.6 multiply_convert_fusion.3
  1055.2 29.8 %fusion.11 = f32[128,2048]{1,0:T(8,128)} fusion(bf16[2048,16384]{1,0:T(8,128)(2,1)} %bitcast.111, bf16[128,8192]{1,0:T(8,128)(2,1)} %get-tuple-element.52, bf16[128,8192]{1,0:T(8,128)(2,1)} %get-tuple-element.51), kind=kOutput, calls=%fused_computation.27 | convolution fusion | flops 8598323200 | bytes 72351744 | tf_op jit(solution)/shard_map/dot_general | solution.py:29
  1103.6 13.3 reduce.4
  1125.4 8.2 all-to-all-done.4
  1141.0 6.0 fusion.7
  1147.0 7.3 multiply_reduce_fusion
  1156.2 7.5 multiply_reduce_fusion.1
  1163.7 5.7 fusion.72
  1185.0 7.0 multiply_convert_fusion.1
  1193.4 5.8 multiply_convert_fusion
  1298.5 13.9 convolution_add_fusion.14
  1314.6 10.4 fusion.57
  1326.5 28.7 %reduce-scatter.7.cloned.1.call-done = bf16[5,128,128]{2,1,0:T(8,128)(2,1)} async-done(((bf16[5,2048,128]{2,1,0:T(8,128)(2,1)}), bf16[5,128,128]{2,1,0:T(8,128)(2,1)}) %reduce-scatter.7.cloned.1.call-update) | async-done | bytes 163856 | tf_op jit(solution)/shard_map/reduce_scatter | solution.py:433
  1355.2 78.9 %reduce-scatter.5.cloned.1.call-done = bf16[6,128,128]{2,1,0:T(8,128)(2,1)} async-done(((bf16[6,2048,128]{2,1,0:T(8,128)(2,1)}), bf16[6,128,128]{2,1,0:T(8,128)(2,1)}) %reduce-scatter.5.cloned.1.call-update) | async-done | bytes 196624 | tf_op jit(solution)/shard_map/reduce_scatter | solution.py:430
  1434.1 80.5 %reduce-scatter.11.cloned.1.call-done = bf16[2,512,128]{2,1,0:T(8,128)(2,1)} async-done(((bf16[2,8192,128]{2,1,0:T(8,128)(2,1)}), bf16[2,512,128]{2,1,0:T(8,128)(2,1)}) %reduce-scatter.11.cloned.1.call-update) | async-done | bytes 262160 | tf_op jit(solution)/shard_map/reduce_scatter | solution.py:439
  1515.9 62.3 %all-reduce.3.cloned.1.call-done = (bf16[6,128,128]{2,1,0:T(8,128)(2,1)}, bf16[5,128,128]{2,1,0:T(8,128)(2,1)}, bf16[1,512,128]{2,1,0:T(8,128)(2,1)}, bf16[2,512,128]{2,1,0:T(8,128)(2,1)}) async-done(((bf16[6,128,128]{2,1,0:T(8,128)(2,1)}, bf16[5,128,128]{2,1,0:T(8,128)(2,1)}, bf16[1,512,128]{2,1,0:T(8,128)(2,1)}, bf16[2,512,128]{2,1,0:T(8,128)(2,1)}), (bf16[6,128,128]{2,1,0:T(8,128)(2,1)}, ...) | async-done | bytes 753680 | tf_op jit(solution)/shard_map/psum | solution.py:444
  (331 shorter events, 272.5 us)
Async XLA Ops:
  7.2 53.6 %all-gather.11.cloned.1.call-start = ((), (), s32[]{:S(2)}) async-start(), calls=%async_computation.13 | async-start | bytes 3342336 | tf_op jit(solution)/shard_map/all_gather | solution.py:206
  7.9 217.7 %all-gather.9.cloned.1.call-start = ((), (), s32[]{:S(2)}) async-start(), calls=%async_computation.12 | async-start | bytes 26738688 | tf_op jit(solution)/shard_map/all_gather | solution.py:214
  10.6 262.8 %all-gather.13.cloned.1.call-start = ((), (), s32[]{:S(2)}) async-start(), calls=%async_computation.14 | async-start | bytes 2785280 | tf_op jit(solution)/shard_map/all_gather | solution.py:207
  11.3 392.3 %all-gather.15.cloned.1.call-start = ((), (), s32[]{:S(2)}) async-start(), calls=%async_computation.15 | async-start | bytes 8912896 | tf_op jit(solution)/shard_map/all_gather | solution.py:215
  11.9 532.5 %all-gather.21.cloned.1.call-start = ((), (), s32[]{:S(2)}) async-start(), calls=%async_computation.18 | async-start | bytes 35651584 | tf_op jit(solution)/shard_map/all_gather | solution.py:305
  12.5 578.8 %all-gather.23.cloned.1.call-start = ((), (), s32[]{:S(2)}) async-start(), calls=%async_computation.19 | async-start | bytes 2228224 | tf_op jit(solution)/shard_map/all_gather | solution.py:208
  13.1 948.4 %all-gather.17.cloned.1.call-start = ((), (), s32[]{:S(2)}) async-start(), calls=%async_computation.16 | async-start | bytes 71303168 | tf_op jit(solution)/shard_map/all_gather | solution.py:281
  15.7 1081.8 %copy-start.60 = (s32[128]{0:T(128)}, s32[128]{0:T(128)S(1)}, u32[]{:S(2)}) copy-start(s32[128]{0:T(128)S(1)} %and_select_fusion) | copy-start | bytes 1540
  19.6 1077.9 %copy-start.56 = (s32[128]{0:T(128)}, s32[128]{0:T(128)S(1)}, u32[]{:S(2)}) copy-start(s32[128]{0:T(128)S(1)} %get-tuple-element.87) | copy-start | bytes 1540
  19.8 220.5 %copy-start.54 = (f32[128]{0:T(128)}, f32[128]{0:T(128)S(1)}, u32[]{:S(2)}) copy-start(f32[128]{0:T(128)S(1)} %add_rsqrt_fusion.1) | copy-start | bytes 1540
  20.6 279.0 %copy-start.38 = (f32[128,32]{0,1:T(8,128)}, f32[128,32]{0,1:T(8,128)S(1)}, u32[]{:S(2)}) copy-start(f32[128,32]{0,1:T(8,128)S(1)} %get-tuple-element.90) | copy-start | bytes 49156
  20.6 219.7 %copy-start.36 = (f32[1,2048]{1,0:T(1,128)}, f32[1,2048]{1,0:T(1,128)S(1)}, u32[]{:S(2)}) copy-start(f32[1,2048]{1,0:T(1,128)S(1)} %get-tuple-element.81) | copy-start | bytes 24580
  62.1 211.3 %copy-start.40 = (bf16[128,128]{1,0:T(8,128)(2,1)}, bf16[128,128]{1,0:T(8,128)(2,1)S(1)}, u32[]{:S(2)}) copy-start(bf16[128,128]{1,0:T(8,128)(2,1)S(1)} %fusion.83) | copy-start | bytes 98308
  63.6 232.4 %copy-start.46 = (bf16[128,128]{1,0:T(8,128)(2,1)}, bf16[128,128]{1,0:T(8,128)(2,1)S(1)}, u32[]{:S(2)}) copy-start(bf16[128,128]{1,0:T(8,128)(2,1)S(1)} %fusion.84) | copy-start | bytes 98308
  65.0 228.3 %copy-start.44 = (bf16[128,128]{1,0:T(8,128)(2,1)}, bf16[128,128]{1,0:T(8,128)(2,1)S(1)}, u32[]{:S(2)}) copy-start(bf16[128,128]{1,0:T(8,128)(2,1)S(1)} %fusion.85) | copy-start | bytes 98308
  288.7 31.8 %all-to-all-start = ((bf16[8,2,16384]{2,1,0:T(2,128)(2,1)}), bf16[8,2,16384]{2,1,0:T(2,128)(2,1)S(1)}, u32[]{:S(2)}, u32[]{:S(2)}) async-start(bf16[8,2,16384]{2,1,0:T(2,128)(2,1)} %reshape.634), calls=%async_computation | async-start | bytes 1048576 | tf_op jit(solution)/shard_map/all_to_all | solution.py:263
  320.5 26.4 %all-to-all-start.2 = ((bf16[8,2,16384]{2,1,0:T(2,128)(2,1)}), bf16[8,2,16384]{2,1,0:T(2,128)(2,1)S(1)}, u32[]{:S(2)}, u32[]{:S(2)}) async-start(bf16[8,2,16384]{2,1,0:T(2,128)(2,1)} %reshape.638), calls=%async_computation.2 | async-start | bytes 1048576 | tf_op jit(solution)/shard_map/all_to_all | solution.py:262
  347.0 15.4 all-to-all-start.1
  387.0 13.8 all-to-all-start.3
  390.5 652.9 %all-gather.19.cloned.1.call-start = ((), (), s32[]{:S(2)}) async-start(), calls=%async_computation.17 | async-start | bytes 4456448 | tf_op jit(solution)/shard_map/all_gather | solution.py:209
  411.0 681.0 %copy-start.2 = (f32[128,2048]{1,0:T(8,128)}, f32[128,2048]{1,0:T(8,128)S(1)}, u32[]{:S(2)}) copy-start(f32[128,2048]{1,0:T(8,128)S(1)} %get-tuple-element.101) | copy-start | bytes 3145732
  411.2 605.9 %copy-start.10 = (bf16[128,2048]{1,0:T(8,128)(2,1)}, bf16[128,2048]{1,0:T(8,128)(2,1)S(1)}, u32[]{:S(2)}) copy-start(bf16[128,2048]{1,0:T(8,128)(2,1)S(1)} %multiply_convert_fusion.5) | copy-start | bytes 1572868
  414.2 632.8 %copy-start.51 = (bf16[128,128]{1,0:T(8,128)(2,1)}, bf16[128,128]{1,0:T(8,128)(2,1)S(1)}, u32[]{:S(2)}) copy-start(bf16[128,128]{1,0:T(8,128)(2,1)S(1)} %fusion.87) | copy-start | bytes 98308
  1118.8 14.8 all-to-all-start.4
  1123.2 203.3 %reduce-scatter.9.cloned.1.call-start = ((), (), s32[]{:S(2)}) async-start(), calls=%async_computation.22 | async-start | bytes 2228224 | tf_op jit(solution)/shard_map/reduce_scatter | solution.py:436
  1180.4 39.7 %all-to-all-start.7 = ((bf16[8,2,16384]{2,1,0:T(2,128)(2,1)}), bf16[8,2,16384]{2,1,0:T(2,128)(2,1)}, u32[]{:S(2)}, u32[]{:S(2)}) async-start(bf16[8,2,16384]{2,1,0:T(2,128)(2,1)} %reshape.644), calls=%async_computation.7 | async-start | bytes 1048576 | tf_op jit(solution)/shard_map/all_to_all | solution.py:369
  1220.1 19.9 %all-to-all-start.6 = ((bf16[8,2,16384]{2,1,0:T(2,128)(2,1)}), bf16[8,2,16384]{2,1,0:T(2,128)(2,1)}, u32[]{:S(2)}, u32[]{:S(2)}) async-start(bf16[8,2,16384]{2,1,0:T(2,128)(2,1)} %reshape.646), calls=%async_computation.6 | async-start | bytes 1048576 | tf_op jit(solution)/shard_map/all_to_all | solution.py:366
  1240.0 23.2 %all-to-all-start.5 = ((bf16[8,2,16384]{2,1,0:T(2,128)(2,1)}), bf16[8,2,16384]{2,1,0:T(2,128)(2,1)}, u32[]{:S(2)}, u32[]{:S(2)}) async-start(bf16[8,2,16384]{2,1,0:T(2,128)(2,1)} %reshape.648), calls=%async_computation.5 | async-start | bytes 1048576 | tf_op jit(solution)/shard_map/all_to_all | solution.py:363
  1244.8 110.4 %reduce-scatter.7.cloned.1.call-start = ((), (), s32[]{:S(2)}) async-start(), calls=%async_computation.21 | async-start | bytes 2785280 | tf_op jit(solution)/shard_map/reduce_scatter | solution.py:433
  1279.4 154.7 %reduce-scatter.5.cloned.1.call-start = ((), (), s32[]{:S(2)}) async-start(), calls=%async_computation.20 | async-start | bytes 3342336 | tf_op jit(solution)/shard_map/reduce_scatter | solution.py:430
  1292.7 221.9 %reduce-scatter.11.cloned.1.call-start = ((), (), s32[]{:S(2)}) async-start(), calls=%async_computation.23 | async-start | bytes 4456448 | tf_op jit(solution)/shard_map/reduce_scatter | solution.py:439
  1298.4 279.9 %all-reduce.3.cloned.1.call-start = ((), (), s32[]{:S(2)}) async-start(), calls=%async_computation.24 | async-start | bytes 1507328 | tf_op jit(solution)/shard_map/psum | solution.py:444
  (57 other events, 460.3 us)
Sparse Core Ops, SparseCore 0:
  10.1 50.5 all-gather.10
  62.8 162.7 all-gather.8
  227.7 45.6 all-gather.12
  275.4 70.1 all-gather.14
  347.5 196.8 all-gather.20
  546.4 44.8 all-gather.22
  593.4 368.0 all-gather.16
  963.6 51.3 all-gather.18
  1127.3 74.4 reduce-scatter.8
  1279.5 75.6 reduce-scatter.6
  1358.9 75.1 reduce-scatter.4
  1437.6 76.8 reduce-scatter.10
  1517.2 61.0 all-reduce.2
where the time goes:
time: 1600 us; the launch traced here: 1590 us
  waiting for transfers between devices  1030 us (64%)
  matrix products  241 us (15%)
  local copies, waits for them, and re-layouts  155 us (10%)
  other arithmetic  110 us (7%)
  starting transfers between devices  37.7 us (2%)
  between operations  16.8 us (1%)
    all_gather x1, waiting for transfers between devices, body(): add_weight_piece = lax.all_gather(gate_up_weight, 'fs', axis=0, tiled=True)  365 us
    all_gather x1, waiting for transfers between devices, body(): lax.all_gather(query_key_value_weight, 'fs', axis=0, tiled=True)  161 us
    all_gather x1, waiting for transfers between devices, body(): lax.all_gather(down_weight, 'fs', axis=0, tiled=True)  130 us
    unnamed x161, local copies, waits for them, and re-layouts  102 us
    dot_general x18, matrix products, matrix_product_transposed(): lax.dot_general(left, right, (((1,), (1,)), ((), ())), preferred_element_...  89.1 us
    dot_general x18, matrix products, matrix_product(): return jnp.dot(left, right, preferred_element_type=jnp.float32)  85.8 us
    reduce_scatter x1, waiting for transfers between devices, body(): lax.psum_scatter(local_out_ff.astype(jnp.bfloat16), 'fs', scatter_dimensi...  80.5 us
    reduce_scatter x1, waiting for transfers between devices, body(): lax.psum_scatter(local_in_d.astype(jnp.bfloat16), 'fs', scatter_dimension...  78.9 us
  transfers between devices with their start and end apart: 21, of which 13 were waited for; matrix products, arithmetic and copies ran while one was open for 26% of the time, Pallas kernels for 0%

commit v1 on v0

v1 whole, which is shorter than its diff:
```python
import jax
import jax.numpy as jnp
from jax import lax
from jax.sharding import PartitionSpec as P

HEAD_SIZE = 64
ADAPTER_RANK = 16
NORM_EPS = 1e-05
ROPE_BASE = 130000.0
MASK_FILL = -1e30
BF = jnp.bfloat16
F32 = jnp.float32


def mm(left, right):
    return jnp.dot(left, right, preferred_element_type=F32)


def mm_nt(left, right):
    return lax.dot_general(left, right, (((1,), (1,)), ((), ())), preferred_element_type=F32)


def mm_tn(left, right):
    return lax.dot_general(left, right, (((0,), (0,)), ((), ())), preferred_element_type=F32)


def shift(x, chips):
    return lax.ppermute(x, "sp", [(i, ((i // 2 + chips) % 4) * 2 + i % 2) for i in range(8)])


def swap(x):
    return lax.ppermute(x, "sp", [(i, i ^ 1) for i in range(8)])


def gather_tokens(x):
    near = jnp.concatenate([x, shift(x, -1), shift(x, 2), shift(x, 1)], 0)
    return jnp.concatenate([near, swap(near)], 0)


def scatter_tokens(parts):
    got = swap(parts[1].astype(BF))
    pair = parts[0] + got.astype(F32)
    total = pair[0]
    for d, back in ((1, 1), (2, 2), (3, -1)):
        total = total + shift(pair[d].astype(BF), back).astype(F32)
    return total


def rms_inverse(values):
    return lax.rsqrt(jnp.mean(values * values, -1, keepdims=True) + NORM_EPS)


def norm_back(grad_norm, values, inverse, gain):
    normed = values * inverse
    scaled = grad_norm * gain
    return inverse * (scaled - normed * jnp.mean(scaled * normed, -1, keepdims=True))


def rope_pair(values, cosine, sine):
    half = values.shape[1] // 2
    a, b = values[:, :half], values[:, half:]
    return jnp.concatenate([a * cosine - b * sine, b * cosine + a * sine], 1)


def split_heads(values, paired):
    rows = values.shape[0]
    if paired:
        return values.reshape(rows, 2, 4, 32).transpose(2, 0, 1, 3).reshape(4, rows, 64)
    return values.reshape(rows, 4, 64).transpose(1, 0, 2)


def join_heads(values, paired):
    rows = values.shape[1]
    if paired:
        return values.reshape(4, rows, 2, 32).transpose(1, 2, 0, 3).reshape(rows, 256)
    return values.transpose(1, 0, 2).reshape(rows, 256)


def attend(q, k, v, allowed):
    scores = jnp.einsum("hqd,hkd->hqk", q, k, preferred_element_type=F32) * 0.125
    scores = jnp.where(allowed[None], scores, MASK_FILL)
    top = jnp.max(scores, -1, keepdims=True)
    weights = jnp.exp(scores - top)
    total = jnp.sum(weights, -1, keepdims=True)
    probs = (weights / total).astype(BF)
    out = jnp.einsum("hqk,hkd->hqd", probs, v, preferred_element_type=F32).astype(BF)
    return out, top + jnp.log(total)


def attend_back(q, k, v, grad, log_total, allowed):
    scores = jnp.einsum("hqd,hkd->hqk", q, k, preferred_element_type=F32) * 0.125
    scores = jnp.where(allowed[None], scores, MASK_FILL)
    probs = jnp.exp(scores - log_total)
    grad_probs = jnp.einsum("hqd,hkd->hqk", grad, v, preferred_element_type=F32)
    inner = jnp.sum(probs * grad_probs, -1, keepdims=True)
    grad_scores = (probs * (grad_probs - inner)).astype(BF)
    gq = jnp.einsum("hqk,hkd->hqd", grad_scores, k, preferred_element_type=F32) * 0.125
    gk = jnp.einsum("hqk,hqd->hkd", grad_scores, q, preferred_element_type=F32) * 0.125
    gv = jnp.einsum("hqk,hqd->hkd", probs.astype(BF), grad, preferred_element_type=F32)
    return gq.astype(BF), gk.astype(BF), gv.astype(BF)


def body(
    layer_input,
    output_gradient,
    norm_gain_pair,
    query_key_value_weight,
    output_weight,
    gate_up_weight,
    down_weight,
    adapter_input_model,
    adapter_output_model,
    adapter_input_hidden,
    adapter_output_hidden,
    spans,
    adapter_choice_rows,
):
    f_at, s_at = lax.axis_index("fs"), lax.axis_index("sp")
    y_at, c_at = s_at // 2, s_at % 2
    x_l = layer_input[0]
    og_l = output_gradient[0]
    rows, width = x_l.shape
    tokens = 8 * rows
    gain_one, gain_two = norm_gain_pair[0], norm_gain_pair[1]

    i512 = lax.broadcasted_iota(jnp.int32, (512, 256), 0)
    j256 = lax.broadcasted_iota(jnp.int32, (512, 256), 1)
    source_qk = ((j256 % 128) // 32) * 128 + c_at * 64 + (j256 // 128) * 32 + j256 % 32
    source_v = (j256 // 64) * 128 + c_at * 64 + j256 % 64
    pick_qk = (i512 == source_qk).astype(BF)
    pick_v = (i512 == source_v).astype(BF)
    wide = lax.dynamic_slice(query_key_value_weight, (0, 0, 512 * y_at), (rows, 3, 512))
    pack_one = jnp.concatenate(
        [
            mm(wide[:, 0], pick_qk).astype(BF),
            mm(wide[:, 1], pick_qk).astype(BF),
            mm(wide[:, 2], pick_v).astype(BF),
            adapter_input_model[0],
            adapter_input_model[1],
            adapter_input_model[2],
        ],
        1,
    )
    pieces = [
        lax.dynamic_slice(gate_up_weight, (0, 0, 512 * f + 64 * s_at), (128, 2, 64)) for f in range(16)
    ]
    gate_up = jnp.concatenate(pieces, 2)
    pack_two = jnp.concatenate(
        [
            gate_up[:, 0],
            gate_up[:, 1],
            adapter_input_model[4],
            adapter_input_model[5],
            adapter_output_model[3],
            adapter_output_model[4],
        ],
        1,
    )
    half = lambda a: lax.dynamic_slice_in_dim(a, 64 * c_at, 64, 0)
    eighth = lambda a: lax.dynamic_slice_in_dim(a, 64 * s_at, 64, 0)
    pack_three = jnp.concatenate(
        [
            eighth(down_weight),
            half(output_weight),
            eighth(adapter_input_hidden[0]),
            eighth(adapter_output_hidden[0]),
            eighth(adapter_output_hidden[1]),
            half(adapter_output_model[0]),
            half(adapter_output_model[1]),
            half(adapter_output_model[2]),
            half(adapter_input_model[3]),
        ],
        1,
    )
    all_one = lax.all_gather(pack_one, "fs", axis=0, tiled=True)
    all_two = lax.all_gather(pack_two, "fs", axis=0, tiled=True)
    all_three = lax.all_gather(pack_three, "fs", axis=0, tiled=True)
    w_qkv, a_qkv = all_one[:, :768], all_one[:, 768:]
    w_gu, a_gu, b_o, b_d = all_two[:, :2048], all_two[:, 2048:2304], all_two[:, 2304:2432], all_two[:, 2432:]
    w_d, w_o = all_three[:, :2048], all_three[:, 2048:4096]
    in_ff, out_g, out_u = all_three[:, 4096:4224], all_three[:, 4224:4352], all_three[:, 4352:4480]
    own_b = lax.dynamic_slice(all_three, (256 * y_at, 4480), (256, 384))
    b_q = own_b[:, :128].reshape(4, 2, 32, 128).transpose(1, 0, 2, 3).reshape(256, 128)
    b_k = own_b[:, 128:256].reshape(4, 2, 32, 128).transpose(1, 0, 2, 3).reshape(256, 128)
    b_v = own_b[:, 256:]
    a_o = all_three[:, 4864:4992]

    at = jnp.arange(tokens, dtype=jnp.int32)
    prompt, second = spans[0, 0], spans[0, 0] + spans[0, 1]

    def mask_of(token):
        segment = (token >= prompt).astype(jnp.int32) + (token >= second).astype(jnp.int32)
        chosen = jnp.where(
            segment == 0,
            adapter_choice_rows[0, 0],
            jnp.where(segment == 1, adapter_choice_rows[0, 1], adapter_choice_rows[0, 2]),
        )
        return (chosen[:, None] == jnp.arange(128)[None, :] // ADAPTER_RANK).astype(F32)

    core_of = jnp.where(at < 4 * rows, c_at, 1 - c_at)
    chip_of = (y_at + (at // rows) % 4) % 4
    relative = (chip_of * 2 + core_of) * rows + at % rows
    own_tokens = s_at * rows + jnp.arange(rows, dtype=jnp.int32)
    mask_abs, mask_rel, mask_own = mask_of(at), mask_of(relative), mask_of(own_tokens)
    mask_chip = mask_of(y_at * 256 + jnp.arange(256, dtype=jnp.int32))
    position = at - jnp.where(at >= second, spans[0, 1], 0)
    freq = ROPE_BASE ** (-(jnp.arange(32, dtype=F32) * 2.0 / HEAD_SIZE))
    phase = position.astype(F32)[:, None] * jnp.tile(freq, 4)[None, :]
    cosine, sine = jnp.cos(phase), jnp.sin(phase)
    i_at, j_at = at[:, None], at[None, :]
    allowed = (j_at <= i_at) & ((j_at < prompt) | (j_at >= second) | (i_at < second))

    def absolute(values):
        blocks = values.reshape(2, 4, rows, -1)
        blocks = jnp.where(c_at == 0, blocks, blocks[::-1])
        twice = jnp.concatenate([blocks, blocks], 1)
        turned = lax.dynamic_slice_in_dim(twice, (4 - y_at) % 4, 4, 1)
        return turned.transpose(1, 0, 2, 3).reshape(tokens, -1)

    x_f = x_l.astype(F32)
    inv_one = rms_inverse(x_f)
    n1_l = (x_f * inv_one * gain_one).astype(BF)
    n1 = gather_tokens(n1_l)
    og = gather_tokens(og_l)
    base = absolute(mm(n1, all_one))
    low = (base[:, 768:] * jnp.tile(mask_abs, (1, 3))).astype(BF)
    low_q, low_k, low_v = low[:, :128], low[:, 128:256], low[:, 256:]
    q = rope_pair(base[:, :256] + mm_nt(low_q, b_q), cosine, sine).astype(BF)
    k = rope_pair(base[:, 256:512] + mm_nt(low_k, b_k), cosine, sine).astype(BF)
    v = (base[:, 512:768] + mm_nt(low_v, b_v)).astype(BF)
    qh, kh, vh = split_heads(q, True), split_heads(k, True), split_heads(v, False)
    out_heads, log_total = attend(qh, kh, vh, allowed)
    mix = join_heads(out_heads, False)

    chunk = lambda values, d: lax.dynamic_slice_in_dim(values, 256 * ((y_at + d) % 4), 256, 0)
    chip_mix = [chunk(mix, 0)] + [shift(chunk(mix, d), d) for d in (1, 2, 3)]
    partial = jnp.zeros((256, width + 128), F32)
    w_o_cat = jnp.concatenate([w_o, a_o], 1)
    for d in range(4):
        partial = partial + mm(chip_mix[d], chunk(w_o_cat, -d))
    pair = partial.reshape(2, rows, -1)
    mine = lax.dynamic_index_in_dim(pair, c_at, 0, False)
    other = lax.dynamic_index_in_dim(pair, 1 - c_at, 0, False)
    summed = mine + swap(other.astype(BF)).astype(F32)
    low_o = (summed[:, width:] * mask_own).astype(BF)
    resid = x_f + summed[:, :width] + mm_nt(low_o, b_o)

    inv_two = rms_inverse(resid)
    n2_l = (resid * inv_two * gain_two).astype(BF)
    n2 = gather_tokens(n2_l)
    low_gu = (mm(n2, a_gu) * jnp.tile(mask_rel, (1, 2))).astype(BF)
    low_g, low_u = low_gu[:, :128], low_gu[:, 128:]
    gate = mm(n2, w_gu[:, :1024]) + mm_nt(low_g, out_g)
    up = mm(n2, w_gu[:, 1024:]) + mm_nt(low_u, out_u)
    sig = jax.nn.sigmoid(gate)
    act = gate * sig
    hidden = (act * up).astype(BF)
    down = jnp.concatenate([mm(hidden, w_d), mm(hidden, in_ff)], 1)
    down = scatter_tokens(down.reshape(2, 4, rows, -1))
    low_d = (down[:, width:] * mask_own).astype(BF)
    layer_output = (resid + down[:, :width] + mm_nt(low_d, b_d)).astype(BF)

    glow_d = (mm(og, b_d).astype(BF)) * mask_rel.astype(BF)
    grad_hidden = mm_nt(og, w_d) + mm_nt(glow_d, in_ff)
    grad_gate = (grad_hidden * up * sig * (1.0 + gate * (1.0 - sig))).astype(BF)
    grad_up = (grad_hidden * act).astype(BF)
    grad_gu = jnp.concatenate([grad_gate, grad_up], 1)
    back = jnp.concatenate([mm_nt(grad_gu, w_gu), mm(grad_gate, out_g), mm(grad_up, out_u)], 1)
    back = scatter_tokens(back.reshape(2, 4, rows, -1))
    glow_gu = back[:, width:].astype(BF) * jnp.tile(mask_own, (1, 2)).astype(BF)
    grad_n2 = back[:, :width] + mm_nt(glow_gu, a_gu)
    grad_resid = og_l.astype(F32) + norm_back(grad_n2, resid, inv_two, gain_two)
    grad_attn = grad_resid.astype(BF)

    other_attn = swap(grad_attn)
    chip_attn = jnp.where(
        c_at == 0,
        jnp.concatenate([grad_attn, other_attn], 0),
        jnp.concatenate([other_attn, grad_attn], 0),
    )
    chip_glow = mm(chip_attn, b_o).astype(BF) * mask_chip.astype(BF)
    grad_mix = (mm_nt(chip_attn, w_o) + mm_nt(chip_glow, a_o)).astype(BF)
    parts = []
    for d in range(4):
        columns = lax.dynamic_slice_in_dim(grad_mix, 256 * ((y_at + d) % 4), 256, 1)
        part = jnp.concatenate([columns, chip_glow], 1)
        parts.append(part if d == 0 else shift(part, d))
    stacked = jnp.stack([parts[0], parts[3], parts[2], parts[1]])
    stacked = lax.dynamic_slice_in_dim(jnp.concatenate([stacked, stacked], 0), (4 - y_at) % 4, 4, 0)
    stacked = stacked.reshape(tokens, 384)
    gmix, glow_o = stacked[:, :256], stacked[:, 256:]

    gqh, gkh, gvh = attend_back(qh, kh, vh, split_heads(gmix, False), log_total, allowed)
    gq = rope_pair(join_heads(gqh, True).astype(F32), cosine, -sine).astype(BF)
    gk = rope_pair(join_heads(gkh, True).astype(F32), cosine, -sine).astype(BF)
    gv = join_heads(gvh, False)
    gqkv = jnp.concatenate([gq, gk, gv], 1)
    back = jnp.concatenate([mm_nt(gqkv, w_qkv), mm(gq, b_q), mm(gk, b_k), mm(gv, b_v)], 1)
    back = back.reshape(4, 2, rows, -1).transpose(1, 0, 2, 3)
    back = jnp.where(c_at == 0, back, back[::-1])
    back = lax.dynamic_slice_in_dim(jnp.concatenate([back, back], 1), y_at, 4, 1)
    back = scatter_tokens(back)
    glow_qkv = back[:, width:].astype(BF) * jnp.tile(mask_own, (1, 3)).astype(BF)
    grad_n1 = back[:, :width] + mm_nt(glow_qkv, a_qkv)
    grad_in = grad_resid + norm_back(grad_n1, x_f, inv_one, gain_one)

    by_token = jnp.concatenate(
        [
            mm_tn(n1_l, glow_qkv),
            mm_tn(n2_l, glow_gu),
            mm_tn(grad_attn, low_o),
            mm_tn(og_l, low_d),
        ],
        1,
    ).astype(BF)
    by_token = by_token.reshape(16, 8, 16, 7, 128).transpose(1, 3, 0, 2, 4)
    by_token = lax.all_to_all(by_token, "sp", split_axis=0, concat_axis=0, tiled=False)
    by_token = jnp.sum(by_token.astype(F32), 0).astype(BF)
    own_q = mm_tn(gq, low_q).reshape(2, 4, 32, 128).transpose(1, 0, 2, 3).reshape(4, 64, 128)
    own_k = mm_tn(gk, low_k).reshape(2, 4, 32, 128).transpose(1, 0, 2, 3).reshape(4, 64, 128)
    own_v = mm_tn(gv, low_v).reshape(4, 64, 128)
    own_o = mm_tn(mix, glow_o).reshape(4, 64, 128)
    own = jnp.concatenate([own_o, own_q, own_k, own_v], 1).astype(BF)
    own = lax.dynamic_update_slice(jnp.zeros((16, 256, 128), BF), own, (4 * y_at, 0, 0))
    feed = jnp.concatenate(
        [
            mm_tn(hidden, glow_d).reshape(16, 64, 128),
            mm_tn(grad_gate, low_g).reshape(16, 64, 128),
            mm_tn(grad_up, low_u).reshape(16, 64, 128),
        ],
        1,
    ).astype(BF)
    everything = jnp.concatenate(
        [by_token.transpose(1, 0, 2, 3).reshape(16, 7 * 16, 128), feed, own], 1
    )
    everything = lax.all_to_all(everything, "fs", split_axis=0, concat_axis=0, tiled=False)
    everything = jnp.sum(everything.astype(F32), 0).astype(BF)
    everything = lax.all_gather(everything, "sp", axis=0, tiled=False).astype(F32)
    by_token = everything[:, :112].reshape(8, 7, 16, 128).transpose(1, 0, 2, 3).reshape(7, 128, 128)
    feed = everything[:, 112:304].reshape(8, 3, 64, 128).transpose(1, 0, 2, 3).reshape(3, 512, 128)
    own = lax.dynamic_slice_in_dim(everything[:, 304:], 2 * (f_at // 4), 2, 0)
    own = own.reshape(2, 4, 64, 128).transpose(1, 0, 2, 3).reshape(4, 128, 128)
    grad_in_d = jnp.concatenate([by_token[:3], own[:1], by_token[3:5]], 0)
    grad_out_d = jnp.concatenate([own[1:], by_token[5:]], 0)
    return (layer_output[None], grad_in[None], grad_in_d, grad_out_d, feed[:1], feed[1:])


def solution(mesh):
    in_specs = (
        P("fs", "sp", None),
        P("fs", "sp", None),
        P(),
        P("fs", None, None),
        P("fs", None),
        P("fs", None, None),
        P("fs", None),
        P(None, "fs", None),
        P(None, "fs", None),
        P(None, "fs", None),
        P(None, "fs", None),
        P("fs", None),
        P("fs", None),
    )
    out_specs = (
        P("fs", "sp", None),
        P("fs", "sp", None),
        P(None, "fs", None),
        P(None, "fs", None),
        P(None, "fs", None),
        P(None, "fs", None),
    )
    return jax.shard_map(body, mesh=mesh, in_specs=in_specs, out_specs=out_specs, check_vma=False)
```

time: 1600 us -> 708 us (0.44)
  waiting for transfers between devices: 1030 us -> 233 us
  matrix products: 241 us -> 147 us
  local copies, waits for them, and re-layouts: 155 us -> 102 us
  blocking collectives: 0 us -> 35.6 us
    all_gather x8 -> x4, waiting for transfers between devices: 758 us -> 74.8 us  [the longest x1 31.8 us: body(): all_two = lax.all_gather(pack_two, 'fs', axis=0, tiled=True)]
    reduce_scatter x4 -> x0, waiting for transfers between devices: 188 us -> none  [the longest x1 80.5 us: body(): lax.psum_scatter(local_out_ff.astype(jnp.bfloat16), 'fs', scatter_dimensi...]
    ppermute x0 -> x32, waiting for transfers between devices: none -> 126 us  [the longest x24 125 us: shift(): lax.ppermute(x, 'sp', [(i, (i // 2 + chips) % 4 * 2 + i % 2) for i in ran...]
    dot_general x62 -> x52, matrix products: 241 us -> 147 us  [the longest x20 50.2 us: mm(): return jnp.dot(left, right, preferred_element_type=F32)]
    unnamed x161 -> x237, local copies, waits for them, and re-layouts: 102 us -> 25.4 us
    psum x1 -> x0, waiting for transfers between devices: 62.3 us -> none  [body(): lax.psum(shard_sums[0].astype(jnp.bfloat16), 'sp').astype(jnp.float32)]
    unnamed x10, other arithmetic: 67.8 us -> 10.3 us
    ppermute x0 -> x32, starting transfers between devices: none -> 40.8 us  [the longest x24 39.2 us: shift(): lax.ppermute(x, 'sp', [(i, (i // 2 + chips) % 4 * 2 + i % 2) for i in ran...]
  transfers between devices with their start and end apart: 21 -> 37, of which waited for: 13 -> 20; matrix products, arithmetic and copies ran while one was open for 26% -> 36% of each run, Pallas kernels for 0% -> 0%
where the time goes in v1:
time: 708 us; the launch traced here: 697 us
  waiting for transfers between devices  233 us (33%)
  matrix products  147 us (21%)
  other arithmetic  115 us (16%)
  local copies, waits for them, and re-layouts  102 us (14%)
  starting transfers between devices  45.9 us (6%)
  blocking collectives  35.6 us (5%)
  between operations  18.1 us (3%)
    ppermute x24, waiting for transfers between devices, shift(): lax.ppermute(x, 'sp', [(i, (i // 2 + chips) % 4 * 2 + i % 2) for i in ran...  125 us
    dot_general x20, matrix products, mm(): return jnp.dot(left, right, preferred_element_type=F32)  50.2 us
    dot_general x15, matrix products, mm_nt(): lax.dot_general(left, right, (((1,), (1,)), ((), ())), preferred_element_...  44.1 us
    ppermute x24, starting transfers between devices, shift(): lax.ppermute(x, 'sp', [(i, (i // 2 + chips) % 4 * 2 + i % 2) for i in ran...  39.2 us
    all_to_all x1, blocking collectives, body(): lax.all_to_all(everything, 'fs', split_axis=0, concat_axis=0, tiled=False)  35.6 us
    all_to_all x1, waiting for transfers between devices, body(): lax.all_to_all(by_token, 'sp', split_axis=0, concat_axis=0, tiled=False)  31.9 us
    all_gather x1, waiting for transfers between devices, body(): all_two = lax.all_gather(pack_two, 'fs', axis=0, tiled=True)  31.8 us
    all_gather x1, waiting for transfers between devices, body(): all_three = lax.all_gather(pack_three, 'fs', axis=0, tiled=True)  30.4 us
  transfers between devices with their start and end apart: 37, of which 20 were waited for; matrix products, arithmetic and copies ran while one was open for 36% of the time, Pallas kernels for 0%

profile of v1, /device:TPU:0, one launch (start us, length us, event | category | flops | bytes accessed | tf_op | source)
XLA Modules:
  0.0 697.0 jit_solution(15229165266657080688)
XLA Ops:
  43.3 17.3 %collective-permute-done.2 = bf16[128,2048]{1,0:T(8,128)(2,1)S(1)} collective-permute-done((bf16[128,2048]{1,0:T(8,128)(2,1)S(1)}, bf16[128,2048]{1,0:T(8,128)(2,1)S(1)}, u32[]{:S(2)}, u32[]{:S(2)}) %collective-permute-start.2) | collective-permute-done | bytes 524320 | tf_op jit(solution)/shard_map/ppermute | solution.py:28
  63.5 9.6 %collective-permute-done.1 = bf16[128,2048]{1,0:T(8,128)(2,1)} collective-permute-done((bf16[128,2048]{1,0:T(8,128)(2,1)S(1)}, bf16[128,2048]{1,0:T(8,128)(2,1)}, u32[]{:S(2)}, u32[]{:S(2)}) %collective-permute-start.1) | collective-permute-done | bytes 524320 | tf_op jit(solution)/shard_map/ppermute | solution.py:28
  93.4 9.0 %fusion.281 = f32[1024,1152]{1,0:T(8,128)S(1)} fusion(bf16[1024,2048]{1,0:T(8,128)(2,1)} %constant_dynamic-update-slice_fusion, bf16[2048,1152]{1,0:T(8,128)(2,1)} %all-gather.6.cloned.1.call-done), kind=kOutput, calls=%fused_computation.494 | convolution fusion | flops 4831838208 | bytes 13631488 | tf_op jit(solution)/shard_map/dot_general | solution.py:16
  105.6 8.2 %copy.180 = f32[4,2,128,1152]{2,1,0,3:T(2,128)} copy(f32[4,2,128,1152]{3,2,0,1:T(8,128)} %fusion.11) | data formatting | bytes 9437184 | tf_op jit(solution)/shard_map/transpose | solution.py:218
  113.8 7.3 %reshape.504 = f32[1024,1152]{0,1:T(8,128)} reshape(f32[4,2,128,1152]{2,1,0,3:T(2,128)} %copy.180) | data formatting | bytes 9437184 | tf_op jit(solution)/shard_map/reshape | solution.py:218
  122.7 30.4 %all-gather.8.cloned.1.call-done = bf16[1024,4992]{1,0:T(8,128)(2,1)} async-done(((bf16[64,4992]{1,0:T(8,128)(2,1)}), bf16[1024,4992]{1,0:T(8,128)(2,1)}) %all-gather.8.cloned.1.call-update) | async-done | bytes 10223632 | tf_op jit(solution)/shard_map/all_gather | solution.py:177
  161.6 7.7 %fusion.280 = (f32[4,1024]{1,0:T(4,128)S(1)}, f32[4,1024,1024]{1,2,0:T(8,128)}) fusion(bf16[4,1024,64]{1,2,0:T(8,128)(2,1)S(1)} %bitcast.318, bf16[4,1024,64]{1,2,0:T(8,128)(2,1)S(1)} %bitcast.316, pred[1024,1024]{0,1:T(8,128)(4,1)S(1)} %fusion.23), kind=kOutput, calls=%fused_computation.493 | convolution fusion | flops 549449728 | bytes 18890752 | tf_op jit(solution)/shard_map/hqd,hkd->hqk/dot_general | solution.py:80
  169.3 8.3 %fusion = f32[4,1024]{1,0:T(4,128)S(1)} fusion(f32[4,1024,1024]{1,2,0:T(8,128)} %get-tuple-element.91, f32[4,1024]{1,0:T(4,128)S(1)} %get-tuple-element.90), kind=kLoop, calls=%fused_computation.9 | loop fusion | flops 8384512 | bytes 16809984 | tf_op jit(solution)/shard_map/reduce_sum | solution.py:84
  177.6 7.5 %fusion.55 = bf16[4,1024,64]{1,2,0:T(8,128)(2,1)S(1)} fusion(bf16[4,1024,64]{1,2,0:T(8,128)(2,1)S(1)} %bitcast.334, f32[4,1024,1024]{1,2,0:T(8,128)} %get-tuple-element.91, f32[4,1024]{1,0:T(4,128)S(1)} %fusion, f32[4,1024]{1,0:T(4,128)S(1)} %get-tuple-element.90), kind=kOutput, calls=%fused_computation.103 | convolution fusion | flops 549715968 | bytes 17858560 | tf_op jit(solution)/shard_map/hqk,hkd->hqd/dot_general | solution.py:86
  203.6 31.8 %all-gather.10.cloned.1.call-done = bf16[2048,2560]{1,0:T(8,128)(2,1)} async-done(((bf16[128,2560]{1,0:T(8,128)(2,1)}), bf16[2048,2560]{1,0:T(8,128)(2,1)}) %all-gather.10.cloned.1.call-update) | async-done | bytes 10485776 | tf_op jit(solution)/shard_map/all_gather | solution.py:176
  252.7 12.0 %collective-permute-done.9 = bf16[128,2048]{1,0:T(8,128)(2,1)S(1)} collective-permute-done((bf16[128,2048]{1,0:T(8,128)(2,1)S(1)}, bf16[128,2048]{1,0:T(8,128)(2,1)S(1)}, u32[]{:S(2)}, u32[]{:S(2)}) %collective-permute-start.9) | collective-permute-done | bytes 524320 | tf_op jit(solution)/shard_map/ppermute | solution.py:28
  266.9 8.4 %fusion.32 = f32[1024,1024]{0,1:T(8,128)} fusion(f32[1024,1024]{0,1:T(8,128)S(1)} %fusion.167, bf16[1024,2048]{1,0:T(8,128)(2,1)S(1)} %constant_dynamic-update-slice_fusion.24, bf16[1024,4992]{1,0:T(8,128)(2,1)} %all-gather.8.cloned.1.call-done), kind=kOutput, calls=%fused_computation.77 | convolution fusion | flops 4296015872 | bytes 16777216 | tf_op jit(solution)/shard_map/dot_general | solution.py:20
  282.8 8.3 %fusion.38 = f32[1024,1024]{0,1:T(8,128)} fusion(f32[1024,1024]{0,1:T(8,128)S(1)} %fusion.173, bf16[1024,2048]{1,0:T(8,128)(2,1)S(1)} %constant_dynamic-update-slice_fusion.19, bf16[2048,2560]{1,0:T(8,128)(2,1)} %all-gather.10.cloned.1.call-done), kind=kOutput, calls=%fused_computation.79 | convolution fusion | flops 4296015872 | bytes 16777216 | tf_op jit(solution)/shard_map/dot_general | solution.py:16
  291.1 11.2 %multiply_convert_fusion.2 = (bf16[1024,1024]{0,1:T(8,128)(2,1)S(1)}, bf16[1024,1024]{0,1:T(8,128)(2,1)S(1)}, bf16[1024,1024]{0,1:T(8,128)(2,1)}) fusion(f32[1024,1024]{0,1:T(8,128)} %fusion.32, f32[1024,1024]{0,1:T(8,128)} %fusion.38, f32[1024,1024]{0,1:T(8,128)S(1)} %fusion.179, bf16[1024,2048]{1,0:T(8,128)(2,1)S(1)} %constant_dynamic-update-slice_fusion.19, ...), kind=kOutput, calls=%fused_computation.51 | convolution fusion | flops 4311744512 | bytes 27262976 | tf_op jit(solution)/shard_map/dot_general | solution.py:16
  306.7 11.3 %fusion.5 = f32[1024,2048]{1,0:T(8,128)S(1)} fusion(bf16[2048,2560]{1,0:T(8,128)(2,1)} %all-gather.10.cloned.1.call-done, bf16[1024,1024]{0,1:T(8,128)(2,1)S(1)} %get-tuple-element.27, bf16[1024,1024]{0,1:T(8,128)(2,1)S(1)} %get-tuple-element.26), kind=kOutput, calls=%fused_computation.24 | convolution fusion | flops 8598323200 | bytes 20971520 | tf_op jit(solution)/shard_map/dot_general | solution.py:20
  343.9 7.1 %collective-permute-done.21 = bf16[128,2304]{1,0:T(8,128)(2,1)S(1)} collective-permute-done((bf16[128,2304]{1,0:T(8,128)(2,1)S(1)}, bf16[128,2304]{1,0:T(8,128)(2,1)S(1)}, u32[]{:S(2)}, u32[]{:S(2)}) %collective-permute-start.21) | collective-permute-done | bytes 589856 | tf_op jit(solution)/shard_map/ppermute | solution.py:28
  351.0 11.5 %collective-permute-done.23 = bf16[128,2304]{1,0:T(8,128)(2,1)S(1)} collective-permute-done((bf16[128,2304]{1,0:T(8,128)(2,1)S(1)}, bf16[128,2304]{1,0:T(8,128)(2,1)S(1)}, u32[]{:S(2)}, u32[]{:S(2)}) %collective-permute-start.23) | collective-permute-done | bytes 589856 | tf_op jit(solution)/shard_map/ppermute | solution.py:28
  380.6 7.9 %collective-permute-done.26 = bf16[256,384]{1,0:T(8,128)(2,1)S(1)} collective-permute-done((bf16[256,384]{1,0:T(8,128)(2,1)S(1)}, bf16[256,384]{1,0:T(8,128)(2,1)S(1)}, u32[]{:S(2)}, u32[]{:S(2)}) %collective-permute-start.26) | collective-permute-done | bytes 196640 | tf_op jit(solution)/shard_map/ppermute | solution.py:28
  393.4 9.2 %fusion.49 = bf16[4,1024,64]{1,2,0:T(8,128)(2,1)} fusion(bf16[4,1024,64]{1,2,0:T(8,128)(2,1)S(1)} %bitcast.320, f32[4,1024,1024]{1,2,0:T(8,128)} %get-tuple-element.91, f32[4,1024]{1,0:T(4,128)S(1)} %log_add_fusion), kind=kOutput, calls=%fused_computation.99 | convolution fusion | flops 545521664 | bytes 17842176 | tf_op jit(solution)/shard_map/hqk,hqd->hkd/dot_general | solution.py:99
  402.6 11.1 %multiply_reduce_fusion = (f32[4,1024]{1,0:T(4,128)S(1)}, f32[4,1024,1024]{1,2,0:T(8,128)}) fusion(f32[4,1024,1024]{1,2,0:T(8,128)} %get-tuple-element.91, f32[4,1024]{1,0:T(4,128)S(1)} %log_add_fusion, bf16[4,1024,64]{1,2,0:T(8,128)(2,1)S(1)} %bitcast.321, bf16[4,1024,64]{1,2,0:T(8,128)(2,1)} %bitcast.335), kind=kOutput, calls=%fused_computation.3 | convolution fusion | flops 549449728 | bytes 34635776 | tf_op jit(solution)/shard_map/hqd,hkd->hqk/dot_general | solution.py:94
  413.7 11.8 %multiply_convert_fusion = bf16[4,1024,1024]{1,2,0:T(8,128)(2,1)S(1)} fusion(f32[4,1024,1024]{1,2,0:T(8,128)} %get-tuple-element.97, f32[4,1024,1024]{1,2,0:T(8,128)} %get-tuple-element.91, f32[4,1024]{1,0:T(4,128)S(1)} %get-tuple-element.96, f32[4,1024]{1,0:T(4,128)S(1)} %log_add_fusion), kind=kLoop, calls=%fused_computation.2 | loop fusion | flops 16777216 | bytes 41975808 | tf_op jit(solution)/shard_map/convert_element_type | solution.py:96
  450.3 11.7 %reverse_select_fusion = f32[2,4,128,2432]{3,2,1,0:T(8,128)} fusion(f32[2,4,128,2432]{3,2,1,0:T(8,128)} %bitcast.302, pred[]{:T(512)S(6)} %eq.159), kind=kLoop, calls=%fused_computation.8 | loop fusion | flops 2490368 | bytes 19922944 | tf_op jit(solution)/shard_map/jit(_where)/select_n | solution.py:300
  462.0 8.7 %fusion.2 = f32[2,4,128,2432]{3,2,1,0:T(8,128)} fusion(s32[]{:T(128)S(6)} %select_n.424, f32[2,4,128,2432]{3,2,1,0:T(8,128)} %reverse_select_fusion), kind=kLoop, calls=%fused_computation.11 | loop fusion | flops 2490368 | bytes 19922948 | tf_op jit(solution)/shard_map/concatenate | solution.py:301
  474.8 5.6 fusion.271
  485.2 25.0 %collective-permute-done.13 = bf16[128,2176]{1,0:T(8,128)(2,1)} collective-permute-done((bf16[128,2176]{1,0:T(8,128)(2,1)}, bf16[128,2176]{1,0:T(8,128)(2,1)}, u32[]{:S(2)}, u32[]{:S(2)}) %collective-permute-start.13) | collective-permute-done | bytes 557088 | tf_op jit(solution)/shard_map/ppermute | solution.py:28
  524.1 10.2 %collective-permute-done.29 = bf16[128,2432]{1,0:T(8,128)(2,1)S(1)} collective-permute-done((bf16[128,2432]{1,0:T(8,128)(2,1)S(1)}, bf16[128,2432]{1,0:T(8,128)(2,1)S(1)}, u32[]{:S(2)}, u32[]{:S(2)}) %collective-permute-start.29) | collective-permute-done | bytes 622624 | tf_op jit(solution)/shard_map/ppermute | solution.py:28
  534.2 11.9 %collective-permute-done.31 = bf16[128,2432]{1,0:T(8,128)(2,1)S(1)} collective-permute-done((bf16[128,2432]{1,0:T(8,128)(2,1)S(1)}, bf16[128,2432]{1,0:T(8,128)(2,1)S(1)}, u32[]{:S(2)}, u32[]{:S(2)}) %collective-permute-start.31) | collective-permute-done | bytes 622624 | tf_op jit(solution)/shard_map/ppermute | solution.py:28
  551.7 6.1 copy.219
  557.7 8.0 %convert_element_type.421 = bf16[16,8,16,7,128]{4,3,2,1,0:T(8,128)(2,1)} reshape(bf16[2048,896]{1,0:T(8,128)(2,1)} %copy.219) | data formatting | bytes 7340032 | tf_op jit(solution)/shard_map/convert_element_type | solution.py:315
  587.6 31.9 %all-to-all-done = bf16[8,7,16,16,128]{4,3,2,1,0:T(8,128)(2,1)} async-done(((bf16[8,7,16,16,128]{4,3,2,1,0:T(8,128)(2,1)}), bf16[8,7,16,16,128]{4,3,2,1,0:T(8,128)(2,1)}, u32[]{:S(2)}, u32[]{:S(2)}) %all-to-all-start) | async-done | bytes 3670048 | tf_op jit(solution)/shard_map/all_to_all | solution.py:317
  625.8 35.6 %all_to_all.10 = bf16[16,560,128]{2,1,0:T(8,128)(2,1)} all-to-all(bf16[16,560,128]{2,1,0:T(8,128)(2,1)S(1)} %constant_dynamic-update-slice_fusion.34), channel_id=1, replica_groups=mesh['fs'=16,'sp'=8] {'fs'}, dimensions={0} | all-to-all | bytes 4587520 | tf_op jit(solution)/shard_map/all_to_all | solution.py:336
  670.9 12.6 %all-gather.12.cloned.1.call-done = bf16[4480,128]{1,0:T(8,128)(2,1)} async-done(((bf16[560,128]{1,0:T(8,128)(2,1)}), bf16[4480,128]{1,0:T(8,128)(2,1)}) %all-gather.12.cloned.1.call-update) | async-done | bytes 1146896 | tf_op jit(solution)/shard_map/all_gather | solution.py:338
  (474 shorter events, 264.9 us)
Async XLA Ops:
  7.2 86.2 %all-gather.6.cloned.1.call-start = ((), (), s32[]{:S(2)}) async-start(), calls=%async_computation.2 | async-start | bytes 5013504 | tf_op jit(solution)/shard_map/all_gather | solution.py:175
  15.2 137.9 %all-gather.8.cloned.1.call-start = ((), (), s32[]{:S(2)}) async-start(), calls=%async_computation.3 | async-start | bytes 10862592 | tf_op jit(solution)/shard_map/all_gather | solution.py:177
  20.6 214.8 %all-gather.10.cloned.1.call-start = ((), (), s32[]{:S(2)}) async-start(), calls=%async_computation.4 | async-start | bytes 11141120 | tf_op jit(solution)/shard_map/all_gather | solution.py:176
  23.0 58.9 %collective-permute-start.18 = (bf16[128,2048]{1,0:T(8,128)(2,1)S(1)}, bf16[128,2048]{1,0:T(8,128)(2,1)S(1)}, u32[]{:S(2)}, u32[]{:S(2)}) collective-permute-start(bf16[128,2048]{1,0:T(8,128)(2,1)S(1)} %bitcast.306), channel_id=1, source_target_pairs={{0,2},{1,3},{2,4},{3,5},{4,6},{5,7},{6,0},{7,1},{8,10},{9,11},{10,... | collective-permute-start | bytes 1572872 | tf_op jit(solution)/shard_map/ppermute | solution.py:28
  24.8 57.2 %collective-permute-start.17 = (bf16[128,2048]{1,0:T(8,128)(2,1)S(1)}, bf16[128,2048]{1,0:T(8,128)(2,1)}, u32[]{:S(2)}, u32[]{:S(2)}) collective-permute-start(bf16[128,2048]{1,0:T(8,128)(2,1)S(1)} %bitcast.307), channel_id=1, source_target_pairs={{0,4},{1,5},{2,6},{3,7},{4,0},{5,1},{6,2},{7,3},{8,12},{9,13},{10,... | collective-permute-start | bytes 1572872 | tf_op jit(solution)/shard_map/ppermute | solution.py:28
  29.7 30.9 %collective-permute-start.2 = (bf16[128,2048]{1,0:T(8,128)(2,1)S(1)}, bf16[128,2048]{1,0:T(8,128)(2,1)S(1)}, u32[]{:S(2)}, u32[]{:S(2)}) collective-permute-start(bf16[128,2048]{1,0:T(8,128)(2,1)S(1)} %get-tuple-element.23), channel_id=1, source_target_pairs={{0,2},{1,3},{2,4},{3,5},{4,6},{5,7},{6,0},{7,1},{8,10},{9,11},{10,... | collective-permute-start | bytes 1572872 | tf_op jit(solution)/shard_map/ppermute | solution.py:28
  29.7 43.5 %collective-permute-start.1 = (bf16[128,2048]{1,0:T(8,128)(2,1)S(1)}, bf16[128,2048]{1,0:T(8,128)(2,1)}, u32[]{:S(2)}, u32[]{:S(2)}) collective-permute-start(bf16[128,2048]{1,0:T(8,128)(2,1)S(1)} %get-tuple-element.23), channel_id=1, source_target_pairs={{0,4},{1,5},{2,6},{3,7},{4,0},{5,1},{6,2},{7,3},{8,12},{9,13},{10,... | collective-permute-start | bytes 1572872 | tf_op jit(solution)/shard_map/ppermute | solution.py:28
  32.5 40.7 %collective-permute-start = (bf16[128,2048]{1,0:T(8,128)(2,1)S(1)}, bf16[128,2048]{1,0:T(8,128)(2,1)}, u32[]{:S(2)}, u32[]{:S(2)}) collective-permute-start(bf16[128,2048]{1,0:T(8,128)(2,1)S(1)} %get-tuple-element.23), channel_id=1, source_target_pairs={{0,6},{1,7},{2,0},{3,1},{4,2},{5,3},{6,4},{7,5},{8,14},{9,15},{10,... | collective-permute-start | bytes 1572872 | tf_op jit(solution)/shard_map/ppermute | solution.py:28
  60.6 21.4 %collective-permute-start.16 = (bf16[128,2048]{1,0:T(8,128)(2,1)S(1)}, bf16[128,2048]{1,0:T(8,128)(2,1)}, u32[]{:S(2)}, u32[]{:S(2)}) collective-permute-start(bf16[128,2048]{1,0:T(8,128)(2,1)S(1)} %bitcast.308), channel_id=1, source_target_pairs={{0,6},{1,7},{2,0},{3,1},{4,2},{5,3},{6,4},{7,5},{8,14},{9,15},{10,... | collective-permute-start | bytes 1572872 | tf_op jit(solution)/shard_map/ppermute | solution.py:28
  75.9 14.3 %collective-permute-start.3 = (bf16[512,2048]{1,0:T(8,128)(2,1)}, bf16[512,2048]{1,0:T(8,128)(2,1)}, u32[]{:S(2)}, u32[]{:S(2)}) collective-permute-start(bf16[512,2048]{1,0:T(8,128)(2,1)} %pad_maximum_fusion.4), channel_id=1, source_target_pairs={{0,1},{1,0},{2,3},{3,2},{4,5},{5,4},{6,7},{7,6},{8,9},{9,8},{10,11... | collective-permute-start | bytes 6291464 | tf_op jit(solution)/shard_map/ppermute | solution.py:32
  84.9 158.4 %collective-permute-start.19 = (bf16[512,2048]{1,0:T(8,128)(2,1)}, bf16[512,2048]{1,0:T(8,128)(2,1)}, u32[]{:S(2)}, u32[]{:S(2)}) collective-permute-start(bf16[512,2048]{1,0:T(8,128)(2,1)} %pad_maximum_fusion.6), channel_id=1, source_target_pairs={{0,1},{1,0},{2,3},{3,2},{4,5},{5,4},{6,7},{7,6},{8,9},{9,8},{10,11... | collective-permute-start | bytes 6291464 | tf_op jit(solution)/shard_map/ppermute | solution.py:32
  185.2 11.9 %collective-permute-start.5 = (bf16[256,256]{0,1:T(8,128)(2,1)S(1)}, bf16[256,256]{0,1:T(8,128)(2,1)S(1)}, u32[]{:S(2)}, u32[]{:S(2)}) collective-permute-start(bf16[256,256]{0,1:T(8,128)(2,1)S(1)} %get-tuple-element.62), channel_id=1, source_target_pairs={{0,4},{1,5},{2,6},{3,7},{4,0},{5,1},{6,2},{7,3},{8,12},{9,13},{10,... | collective-permute-start | bytes 393224 | tf_op jit(solution)/shard_map/ppermute | solution.py:28
  188.7 7.9 %collective-permute-start.6 = (bf16[256,256]{0,1:T(8,128)(2,1)S(1)}, bf16[256,256]{0,1:T(8,128)(2,1)S(1)}, u32[]{:S(2)}, u32[]{:S(2)}) collective-permute-start(bf16[256,256]{0,1:T(8,128)(2,1)S(1)} %get-tuple-element.63), channel_id=1, source_target_pairs={{0,6},{1,7},{2,0},{3,1},{4,2},{5,3},{6,4},{7,5},{8,14},{9,15},{10,... | collective-permute-start | bytes 393224 | tf_op jit(solution)/shard_map/ppermute | solution.py:28
  237.6 15.1 %collective-permute-start.10 = (bf16[128,2048]{1,0:T(8,128)(2,1)S(1)}, bf16[128,2048]{1,0:T(8,128)(2,1)S(1)}, u32[]{:S(2)}, u32[]{:S(2)}) collective-permute-start(bf16[128,2048]{1,0:T(8,128)(2,1)S(1)} %get-tuple-element.21), channel_id=1, source_target_pairs={{0,2},{1,3},{2,4},{3,5},{4,6},{5,7},{6,0},{7,1},{8,10},{9,11},{10,... | collective-permute-start | bytes 1572872 | tf_op jit(solution)/shard_map/ppermute | solution.py:28
  239.2 25.6 %collective-permute-start.9 = (bf16[128,2048]{1,0:T(8,128)(2,1)S(1)}, bf16[128,2048]{1,0:T(8,128)(2,1)S(1)}, u32[]{:S(2)}, u32[]{:S(2)}) collective-permute-start(bf16[128,2048]{1,0:T(8,128)(2,1)S(1)} %get-tuple-element.21), channel_id=1, source_target_pairs={{0,4},{1,5},{2,6},{3,7},{4,0},{5,1},{6,2},{7,3},{8,12},{9,13},{10,... | collective-permute-start | bytes 1572872 | tf_op jit(solution)/shard_map/ppermute | solution.py:28
  241.9 22.9 %collective-permute-start.8 = (bf16[128,2048]{1,0:T(8,128)(2,1)S(1)}, bf16[128,2048]{1,0:T(8,128)(2,1)S(1)}, u32[]{:S(2)}, u32[]{:S(2)}) collective-permute-start(bf16[128,2048]{1,0:T(8,128)(2,1)S(1)} %get-tuple-element.21), channel_id=1, source_target_pairs={{0,6},{1,7},{2,0},{3,1},{4,2},{5,3},{6,4},{7,5},{8,14},{9,15},{10,... | collective-permute-start | bytes 1572872 | tf_op jit(solution)/shard_map/ppermute | solution.py:28
  265.0 10.5 %collective-permute-start.11 = (bf16[512,2048]{1,0:T(8,128)(2,1)S(1)}, bf16[512,2048]{1,0:T(8,128)(2,1)S(1)}, u32[]{:S(2)}, u32[]{:S(2)}) collective-permute-start(bf16[512,2048]{1,0:T(8,128)(2,1)S(1)} %pad_maximum_fusion.5), channel_id=1, source_target_pairs={{0,1},{1,0},{2,3},{3,2},{4,5},{5,4},{6,7},{7,6},{8,9},{9,8},{10,11... | collective-permute-start | bytes 6291464 | tf_op jit(solution)/shard_map/ppermute | solution.py:32
  334.0 17.0 %collective-permute-start.21 = (bf16[128,2304]{1,0:T(8,128)(2,1)S(1)}, bf16[128,2304]{1,0:T(8,128)(2,1)S(1)}, u32[]{:S(2)}, u32[]{:S(2)}) collective-permute-start(bf16[128,2304]{1,0:T(8,128)(2,1)S(1)} %get-tuple-element.48), channel_id=1, source_target_pairs={{0,2},{1,3},{2,4},{3,5},{4,6},{5,7},{6,0},{7,1},{8,10},{9,11},{10,... | collective-permute-start | bytes 1769480 | tf_op jit(solution)/shard_map/ppermute | solution.py:28
  335.4 27.0 %collective-permute-start.23 = (bf16[128,2304]{1,0:T(8,128)(2,1)S(1)}, bf16[128,2304]{1,0:T(8,128)(2,1)S(1)}, u32[]{:S(2)}, u32[]{:S(2)}) collective-permute-start(bf16[128,2304]{1,0:T(8,128)(2,1)S(1)} %get-tuple-element.49), channel_id=1, source_target_pairs={{0,6},{1,7},{2,0},{3,1},{4,2},{5,3},{6,4},{7,5},{8,14},{9,15},{10,... | collective-permute-start | bytes 1769480 | tf_op jit(solution)/shard_map/ppermute | solution.py:28
  337.3 26.4 %collective-permute-start.22 = (bf16[128,2304]{1,0:T(8,128)(2,1)S(1)}, bf16[128,2304]{1,0:T(8,128)(2,1)S(1)}, u32[]{:S(2)}, u32[]{:S(2)}) collective-permute-start(bf16[128,2304]{1,0:T(8,128)(2,1)S(1)} %get-tuple-element.50), channel_id=1, source_target_pairs={{0,4},{1,5},{2,6},{3,7},{4,0},{5,1},{6,2},{7,3},{8,12},{9,13},{10,... | collective-permute-start | bytes 1769480 | tf_op jit(solution)/shard_map/ppermute | solution.py:28
  377.4 97.4 %collective-permute-start.12 = (bf16[4,128,2176]{2,1,0:T(8,128)(2,1)}, bf16[4,128,2176]{2,1,0:T(8,128)(2,1)}, u32[]{:S(2)}, u32[]{:S(2)}) collective-permute-start(bf16[4,128,2176]{2,1,0:T(8,128)(2,1)} %bitcast.54), channel_id=1, source_target_pairs={{0,1},{1,0},{2,3},{3,2},{4,5},{5,4},{6,7},{7,6},{8,9},{9,8},{10,11... | collective-permute-start | bytes 6684680 | tf_op jit(solution)/shard_map/ppermute | solution.py:32
  377.6 12.5 %collective-permute-start.27 = (bf16[256,384]{1,0:T(8,128)(2,1)S(1)}, bf16[256,384]{1,0:T(8,128)(2,1)S(1)}, u32[]{:S(2)}, u32[]{:S(2)}) collective-permute-start(bf16[256,384]{1,0:T(8,128)(2,1)S(1)} %get-tuple-element.76), channel_id=1, source_target_pairs={{0,2},{1,3},{2,4},{3,5},{4,6},{5,7},{6,0},{7,1},{8,10},{9,11},{10,... | collective-permute-start | bytes 589832 | tf_op jit(solution)/shard_map/ppermute | solution.py:28
  377.6 10.9 %collective-permute-start.26 = (bf16[256,384]{1,0:T(8,128)(2,1)S(1)}, bf16[256,384]{1,0:T(8,128)(2,1)S(1)}, u32[]{:S(2)}, u32[]{:S(2)}) collective-permute-start(bf16[256,384]{1,0:T(8,128)(2,1)S(1)} %get-tuple-element.78), channel_id=1, source_target_pairs={{0,4},{1,5},{2,6},{3,7},{4,0},{5,1},{6,2},{7,3},{8,12},{9,13},{10,... | collective-permute-start | bytes 589832 | tf_op jit(solution)/shard_map/ppermute | solution.py:28
  474.8 37.4 %collective-permute-start.28 = (bf16[4,128,2432]{2,1,0:T(8,128)(2,1)}, bf16[4,128,2432]{2,1,0:T(8,128)(2,1)}, u32[]{:S(2)}, u32[]{:S(2)}) collective-permute-start(bf16[4,128,2432]{2,1,0:T(8,128)(2,1)} %fusion.30), channel_id=1, source_target_pairs={{0,1},{1,0},{2,3},{3,2},{4,5},{5,4},{6,7},{7,6},{8,9},{9,8},{10,11... | collective-permute-start | bytes 7471112 | tf_op jit(solution)/shard_map/ppermute | solution.py:32
  481.7 28.5 %collective-permute-start.13 = (bf16[128,2176]{1,0:T(8,128)(2,1)}, bf16[128,2176]{1,0:T(8,128)(2,1)}, u32[]{:S(2)}, u32[]{:S(2)}) collective-permute-start(bf16[128,2176]{1,0:T(8,128)(2,1)} %get-tuple-element.51), channel_id=1, source_target_pairs={{0,2},{1,3},{2,4},{3,5},{4,6},{5,7},{6,0},{7,1},{8,10},{9,11},{10,... | collective-permute-start | bytes 1671176 | tf_op jit(solution)/shard_map/ppermute | solution.py:28
  481.7 28.5 %collective-permute-start.15 = (bf16[128,2176]{1,0:T(8,128)(2,1)}, bf16[128,2176]{1,0:T(8,128)(2,1)}, u32[]{:S(2)}, u32[]{:S(2)}) collective-permute-start(bf16[128,2176]{1,0:T(8,128)(2,1)} %get-tuple-element.52), channel_id=1, source_target_pairs={{0,6},{1,7},{2,0},{3,1},{4,2},{5,3},{6,4},{7,5},{8,14},{9,15},{10,... | collective-permute-start | bytes 1671176 | tf_op jit(solution)/shard_map/ppermute | solution.py:28
  484.9 25.3 %collective-permute-start.14 = (bf16[128,2176]{1,0:T(8,128)(2,1)}, bf16[128,2176]{1,0:T(8,128)(2,1)}, u32[]{:S(2)}, u32[]{:S(2)}) collective-permute-start(bf16[128,2176]{1,0:T(8,128)(2,1)} %get-tuple-element.53), channel_id=1, source_target_pairs={{0,4},{1,5},{2,6},{3,7},{4,0},{5,1},{6,2},{7,3},{8,12},{9,13},{10,... | collective-permute-start | bytes 1671176 | tf_op jit(solution)/shard_map/ppermute | solution.py:28
  516.5 17.7 %collective-permute-start.29 = (bf16[128,2432]{1,0:T(8,128)(2,1)S(1)}, bf16[128,2432]{1,0:T(8,128)(2,1)S(1)}, u32[]{:S(2)}, u32[]{:S(2)}) collective-permute-start(bf16[128,2432]{1,0:T(8,128)(2,1)S(1)} %get-tuple-element.45), channel_id=1, source_target_pairs={{0,2},{1,3},{2,4},{3,5},{4,6},{5,7},{6,0},{7,1},{8,10},{9,11},{10,... | collective-permute-start | bytes 1867784 | tf_op jit(solution)/shard_map/ppermute | solution.py:28
  517.4 28.7 %collective-permute-start.31 = (bf16[128,2432]{1,0:T(8,128)(2,1)S(1)}, bf16[128,2432]{1,0:T(8,128)(2,1)S(1)}, u32[]{:S(2)}, u32[]{:S(2)}) collective-permute-start(bf16[128,2432]{1,0:T(8,128)(2,1)S(1)} %get-tuple-element.46), channel_id=1, source_target_pairs={{0,6},{1,7},{2,0},{3,1},{4,2},{5,3},{6,4},{7,5},{8,14},{9,15},{10,... | collective-permute-start | bytes 1867784 | tf_op jit(solution)/shard_map/ppermute | solution.py:28
  519.8 27.8 %collective-permute-start.30 = (bf16[128,2432]{1,0:T(8,128)(2,1)S(1)}, bf16[128,2432]{1,0:T(8,128)(2,1)S(1)}, u32[]{:S(2)}, u32[]{:S(2)}) collective-permute-start(bf16[128,2432]{1,0:T(8,128)(2,1)S(1)} %get-tuple-element.47), channel_id=1, source_target_pairs={{0,4},{1,5},{2,6},{3,7},{4,0},{5,1},{6,2},{7,3},{8,12},{9,13},{10,... | collective-permute-start | bytes 1867784 | tf_op jit(solution)/shard_map/ppermute | solution.py:28
  570.8 48.7 %all-to-all-start = ((bf16[8,7,16,16,128]{4,3,2,1,0:T(8,128)(2,1)}), bf16[8,7,16,16,128]{4,3,2,1,0:T(8,128)(2,1)}, u32[]{:S(2)}, u32[]{:S(2)}) async-start(bf16[8,7,16,16,128]{4,3,2,1,0:T(8,128)(2,1)} %copy.220), calls=%async_computation | async-start | bytes 7340032 | tf_op jit(solution)/shard_map/all_to_all | solution.py:317
  575.5 108.0 %all-gather.12.cloned.1.call-start = ((), (), s32[]{:S(2)}) async-start(), calls=%async_computation.5 | async-start | bytes 1290240 | tf_op jit(solution)/shard_map/all_gather | solution.py:338
  (100 other events, 1490.3 us)
Sparse Core Ops, SparseCore 0:
  15.4 56.6 all-gather.5
  74.1 78.9 all-gather.7
  155.2 80.0 all-gather.9
  664.2 19.2 all-gather.11

commit v2 on v1

v2 whole, which is shorter than its diff:
```python
import functools

import jax
import jax.numpy as jnp
from jax import lax
from jax.experimental import pallas as pl
from jax.experimental.pallas import tpu as pltpu
from jax.sharding import PartitionSpec as P

HEAD_SIZE = 64
ADAPTER_RANK = 16
NORM_EPS = 1e-05
ROPE_BASE = 130000.0
MASK_FILL = -1e30
BF = jnp.bfloat16
F32 = jnp.float32
WIDTH = 2048
ROWS = 128
ORDER = (2, 1, 3, 0)


def mm(left, right):
    return jnp.dot(left, right, preferred_element_type=F32)


def mm_nt(left, right):
    return lax.dot_general(left, right, (((1,), (1,)), ((), ())), preferred_element_type=F32)


def mm_tn(left, right):
    return lax.dot_general(left, right, (((0,), (0,)), ((), ())), preferred_element_type=F32)


def shift(x, chips):
    return lax.ppermute(x, "sp", [(i, ((i // 2 + chips) % 4) * 2 + i % 2) for i in range(8)])


def swap(x):
    return lax.ppermute(x, "sp", [(i, i ^ 1) for i in range(8)])


def shift_z(x, chips):
    return lax.ppermute(x, "fs", [(i, (i + 4 * chips) % 16) for i in range(16)])


def shift_x(x, chips):
    return lax.ppermute(x, "fs", [(i, i - i % 4 + (i + chips) % 4) for i in range(16)])


Y_LINES = [[0, 2, 4, 6], [1, 3, 5, 7]]


def gather_y(x):
    return lax.all_gather(x, "sp", axis=0, tiled=False, axis_index_groups=Y_LINES)


def exchange_y(x):
    return lax.all_to_all(x, "sp", split_axis=0, concat_axis=0, axis_index_groups=Y_LINES)


def line(x, move):
    return [x, move(x, -1), move(x, 2), move(x, 1)]


VMEM = pl.BlockSpec(memory_space=pltpu.VMEM)
SMEM = pl.BlockSpec(memory_space=pltpu.SMEM)


class Info:
    def __init__(self, spans, choice):
        s_at, f_at = lax.axis_index("sp"), lax.axis_index("fs")
        self.values = [s_at >> 1, s_at & 1]
        if spans is None:
            self.values += [None] * 5
        else:
            self.values += [spans[0, 0], spans[0, 0] + spans[0, 1]] + [choice[0, i] for i in range(3)]
        self.values += [f_at >> 2, f_at & 3]

    def __getitem__(self, index):
        return self.values[index]


def call(kernel, outs, scratch, args, limit, deps=()):
    outs = [jax.ShapeDtypeStruct(shape, dtype) for shape, dtype in outs]
    rows, args = args[0], args[1:]
    first = len(rows)
    count, skip = first + len(args), first + len(args) + len(deps)

    def run(*refs):
        info = Info(*refs[:2]) if rows else Info(None, None)
        kernel(info, *refs[first:count], *refs[skip:])

    return pl.pallas_call(
        run,
        out_shape=outs,
        in_specs=[SMEM] * first + [VMEM] * len(args) + [pl.BlockSpec(memory_space=pl.ANY)] * len(deps),
        out_specs=[VMEM] * len(outs),
        scratch_shapes=[pltpu.VMEM(shape, dtype) for shape, dtype in scratch],
        compiler_params=pltpu.CompilerParams(vmem_limit_bytes=limit << 20),
        cost_estimate=pl.CostEstimate(flops=1 << 10, bytes_accessed=1 << 10, transcendentals=0),
    )(*rows, *args, *deps)


def lane_mask(info, first, rows):
    token = first + lax.broadcasted_iota(jnp.int32, (rows, 128), 0)
    lane = lax.broadcasted_iota(jnp.int32, (rows, 128), 1) // ADAPTER_RANK
    chosen = jnp.where(token < info[2], info[4], jnp.where(token < info[3], info[5], info[6]))
    return lane == chosen


def chip_mask(info, step):
    chip, core = (info[0] + step) % 4, info[1]
    return jnp.concatenate(
        [
            lane_mask(info, (2 * chip + core) * ROWS, ROWS),
            lane_mask(info, (2 * chip + 1 - core) * ROWS, ROWS),
        ],
        0,
    )


def turn(a, b, cosine, sine):
    return a * cosine - b * sine, b * cosine + a * sine


def aligned(index, unit):
    return pl.ds(pl.multiple_of(index, unit), unit)


def own_first(info, block):
    return (block // 2) * 256 + ((info[1] + block) % 2) * ROWS


def pack_kernel(info, w, a_in, a_out, w_o, w_pack, ab_pack):
    y_at, core = info[0], info[1]
    i = lax.broadcasted_iota(jnp.int32, (512, 256), 0)
    j = lax.broadcasted_iota(jnp.int32, (512, 256), 1)
    pick_qk = i == ((j % 128) // 32) * 128 + core * 64 + (j // 128) * 32 + j % 32
    pick_v = i == (j // 64) * 128 + core * 64 + j % 64
    for part, pick in enumerate((pick_qk, pick_qk, pick_v)):
        wide = w[part, :, aligned(512 * y_at, 512)]
        w_pack[:, 256 * part : 256 * part + 256] = mm(wide, pick.astype(BF)).astype(BF)
    half = aligned(64 * core, 64)
    for part in range(3):
        ab_pack[:, 128 * part : 128 * part + 128] = a_in[part]
    ab_pack[:64, 384:512] = a_out[0, half, :]
    ab_pack[64:, 384:512] = a_out[1, half, :]
    ab_pack[:64, 512:640] = a_out[2, half, :]
    ab_pack[64:, 512:640] = a_in[3, half, :]
    ab_pack[:, 640:] = a_out[3]
    for part in range(8):
        lanes = slice(256 * part, 256 * part + 256)
        w_pack[16 * part : 16 * part + 16, 768:] = w_o[aligned(64 * core + 16 * y_at, 16), lanes]


def pack(w, a_in, a_out, w_o):
    return call(
        pack_kernel,
        [((ROWS, 1024), BF), ((ROWS, 768), BF)],
        [],
        ((), w, a_in, a_out, w_o),
        8,
    )


def pack_feed_kernel(info, w_gu, w_d, a_in, a_out, in_ff, out_ff, out):
    y_at, core = info[0], info[1]
    i = lax.broadcasted_iota(jnp.int32, (128, 128), 0)
    j = lax.broadcasted_iota(jnp.int32, (128, 128), 1)
    first = ((j < 64) & (i == j + 64 * core)).astype(BF)
    second = ((j >= 64) & (i == j - 64 + 64 * core)).astype(BF)
    for part in range(2):
        for block in range(8):
            left = w_gu[:, part, aligned(1024 * block + 128 * y_at, 128)]
            right = w_gu[:, part, aligned(1024 * block + 512 + 128 * y_at, 128)]
            lanes = slice(1024 * part + 128 * block, 1024 * part + 128 * block + 128)
            out[:ROWS, lanes] = (mm(left, first) + mm(right, second)).astype(BF)
    out[:ROWS, 2048:2176] = a_in[4]
    out[:ROWS, 2176:2304] = a_in[5]
    out[:ROWS, 2304:] = a_out[4]
    eighth = aligned(64 * (2 * y_at + core), 64)
    out[ROWS:, :WIDTH] = w_d[eighth, :]
    out[ROWS:, 2048:2176] = in_ff[0, eighth, :]
    out[ROWS:, 2176:2304] = out_ff[0, eighth, :]
    out[ROWS:, 2304:] = out_ff[1, eighth, :]


def pack_feed(deps, *args):
    return call(pack_feed_kernel, [((192, 2432), BF)], [], ((), *args), 12, deps)[0]


def stack_rows(deps, *lists):
    counts = [len(parts) for parts in lists]

    def kernel(info, *refs):
        at = 0
        for count, out in zip(counts, refs[sum(counts) :]):
            for i in range(count):
                out[i] = refs[at + i][...]
            at += count

    outs = [((len(parts),) + parts[0].shape, parts[0].dtype) for parts in lists]
    return call(kernel, outs, [], ((), *sum(lists, [])), 8, deps)


def order_chips(parts):
    def kernel(info, *refs):
        for d, part in enumerate(refs[:-1]):
            refs[-1][(info[0] + d) % 4] = part[...]

    return call(kernel, [((4,) + parts[0].shape, parts[0].dtype)], [], ((), *parts), 8)[0]


def stack_output(deps, parts):
    def kernel(info, *refs):
        for i, part in enumerate(refs[:-1]):
            refs[-1][i] = part[:, :, 768:]

    return call(kernel, [((4, 4, ROWS, 256), BF)], [], ((), *parts), 8, deps)[0]


def stack_output(deps, parts):
    def kernel(info, *refs):
        for i, part in enumerate(refs[:-1]):
            refs[-1][i] = part[:, :, 768:]

    return call(kernel, [((4, 4, ROWS, 256), BF)], [], ((), *parts), 8, deps)[0]


def hold(deps, *pairs):
    firsts = [first for _, first in pairs]

    def kernel(info, *refs):
        for first, ref, out in zip(firsts, refs, refs[len(firsts) :]):
            out[...] = ref[first : first + 2]

    arrays = [array for array, _ in pairs]
    outs = [((2,) + array.shape[1:], array.dtype) for array in arrays]
    return call(kernel, outs, [], ((), *arrays), 8, deps)


def norm_kernel(info, x, gain, out):
    values = x[...].astype(F32)
    inverse = lax.rsqrt(jnp.mean(values * values, -1, keepdims=True) + NORM_EPS)
    out[...] = (values * inverse * gain[0:1, :]).astype(BF)


def norm_first(deps, info, x, gain):
    return call(norm_kernel, [((ROWS, WIDTH), BF)], [], (info, x, gain), 4, deps)[0]


def copy_kernel(info, x, out):
    out[...] = x[...]


def copy_after(deps, info, x):
    return call(copy_kernel, [(x.shape, x.dtype)], [], (info, x), 4, deps)[0]


def qkv_kernel(info, a0, a1, a2, a3, b0, b1, b2, b3, near, far, cosine, sine, *refs):
    q, k, v, low_out, n1, w, a, b_q, b_k, b_v, a_o, b_o, rest = refs
    z_at, x_at, y_at, core = info[7], info[8], info[0], info[1]
    for dz in range(4):
        for dx in range(4):
            f = ((z_at + dz) % 4) * 4 + (x_at + dx) % 4
            rows = aligned(f * ROWS, ROWS)
            w[rows, :] = (a0, a1, a2, a3)[dz][dx, :, :768]
            piece = (b0, b1, b2, b3)[dx]
            a[rows, :] = piece[dz, :, :384]
            rest[rows, :] = piece[dz, :, 384:640]
            b_o[rows, :] = piece[dz, :, 640:]
    for head in range(4):
        first = (4 * y_at + head) * ROWS
        for half in range(2):
            to = slice(half * 128 + head * 32, half * 128 + head * 32 + 32)
            b_q[to, :] = rest[aligned(first + 32 * half, 32), :128]
            b_k[to, :] = rest[aligned(first + 64 + 32 * half, 32), :128]
        b_v[64 * head : 64 * head + 64, :] = rest[aligned(first, 64), 128:]
    for f in range(16):
        a_o[64 * f : 64 * f + 64, :] = rest[f * ROWS + 64 : f * ROWS + 128, 128:]
    for block in range(8):
        d, same = block // 2, core == block % 2
        n1[block * ROWS : block * ROWS + ROWS, :] = jnp.where(same, near[d], far[d])
    for chip in range(4):
        at = slice(256 * chip, 256 * chip + 256)
        rows = n1[at, :]
        mask = lane_mask(info, 256 * chip, 256)
        low = jnp.where(jnp.concatenate([mask] * 3, 1), mm(rows, a[...]), 0.0).astype(BF)
        low_out[at, :] = low
        cos, sin = cosine[at, :], sine[at, :]
        for j, (b, out) in enumerate(((b_q, q), (b_k, k))):
            base = mm(rows, w[:, 256 * j : 256 * j + 256])
            values = base + mm_nt(low[:, 128 * j : 128 * j + 128], b[...])
            first, second = turn(values[:, :128], values[:, 128:], cos, sin)
            out[at, :128] = first.astype(BF)
            out[at, 128:] = second.astype(BF)
        v[at, :] = (mm(rows, w[:, 512:]) + mm_nt(low[:, 256:], b_v[...])).astype(BF)


def project_qkv(deps, info, w_parts, ab_parts, near, far, cosine, sine):
    return call(
        qkv_kernel,
        [
            ((1024, 256), BF),
            ((1024, 256), BF),
            ((1024, 256), BF),
            ((1024, 384), BF),
            ((1024, WIDTH), BF),
            ((WIDTH, 768), BF),
            ((WIDTH, 384), BF),
            ((256, 128), BF),
            ((256, 128), BF),
            ((256, 128), BF),
            ((1024, 128), BF),
            ((WIDTH, 128), BF),
        ],
        [((WIDTH, 256), BF)],
        (info, *w_parts, *ab_parts, near, far, cosine, sine),
        16,
        deps,
    )


def head_lanes(head, rows, paired):
    lane = lax.broadcasted_iota(jnp.int32, (rows, 256), 1)
    return ((lane % 128) // 32 if paired else lane // 64) == head


def key_bias(info, block):
    n = 256 * (block + 1)
    j = lax.broadcasted_iota(jnp.int32, (n, 256), 0)
    i = 256 * block + lax.broadcasted_iota(jnp.int32, (n, 256), 1)
    allowed = (j <= i) & ((j < info[2]) | (j >= info[3]) | (i < info[3]))
    return jnp.where(allowed, 0.0, MASK_FILL)


def attend_kernel(info, q, k, v, mix, log_total, v_heads, probs):
    for head in range(4):
        v_heads[head] = jnp.where(head_lanes(head, 1024, False), v[...], 0)
    for block in range(4):
        n = 256 * (block + 1)
        rows = slice(256 * block, 256 * block + 256)
        bias = key_bias(info, block)
        out = jnp.zeros((256, 256), F32)
        for head in range(4):
            q_head = jnp.where(head_lanes(head, 256, True), q[rows, :], 0) * jnp.array(0.125, BF)
            scores = mm_nt(k[:n, :], q_head) + bias
            top = jnp.max(scores, 0, keepdims=True)
            weights = jnp.exp(scores - top)
            total = jnp.sum(weights, 0, keepdims=True)
            log_total[head : head + 1, rows] = top + jnp.log(total)
            probs[head, :n, :] = (weights * (1.0 / total)).astype(BF)
        for head in range(4):
            out = out + mm_tn(probs[head, :n, :], v_heads[head, :n, :])
        out = out.astype(BF)
        for part in range(2):
            row = own_first(info, 2 * block + part)
            mix[aligned(row, ROWS), :] = out[part * ROWS : part * ROWS + ROWS]


def attend(info, q, k, v):
    return call(
        attend_kernel,
        [((1024, 256), BF), ((8, 1024), F32)],
        [((4, 1024, 256), BF), ((4, 1024, 256), BF)],
        (info, q, k, v),
        16,
    )


def attend_back_kernel(
    info, q, k, v, g0, g1, g2, g3, log_total, cosine, sine, out, q_heads, g_heads, k_heads, probs, grads, dk, dv
):
    chip, core = info[0], info[1]
    for d, part in enumerate((g0, g1, g2, g3)):
        block = (chip - d + 4) % 4
        for other in range(2):
            rows = part[other * ROWS : other * ROWS + ROWS, :256]
            second = (core + other) % 2
            for head in range(4):
                g_heads[block, aligned(256 * head + ROWS * second, ROWS), :] = jnp.where(
                    head_lanes(head, ROWS, False), rows, 0
                )
    for head in range(4):
        k_heads[head] = jnp.where(head_lanes(head, 1024, True), k[...], 0) * jnp.array(0.125, BF)
    dk[...] = jnp.zeros_like(dk)
    dv[...] = jnp.zeros_like(dv)

    def unrotate(values, rows):
        a, b = values[:, :128].astype(F32), values[:, 128:].astype(F32)
        first, last = turn(a, b, cosine[rows, :], -sine[rows, :])
        return jnp.concatenate([first, last], 1).astype(BF)

    for block in range(4):
        n = 256 * (block + 1)
        rows = slice(256 * block, 256 * block + 256)
        bias = key_bias(info, block)
        for head in range(4):
            at = slice(256 * head, 256 * head + 256)
            q_head = jnp.where(head_lanes(head, 256, True), q[rows, :], 0) * jnp.array(0.125, BF)
            q_heads[at, :] = q_head
            scores = mm_nt(k[:n, :], q_head) + bias
            p = jnp.exp(scores - log_total[head : head + 1, rows])
            dp = mm_nt(v[:n, :], g_heads[block, at, :])
            inner = jnp.sum(p * dp, 0, keepdims=True)
            probs[:n, at] = p.astype(BF)
            grads[:n, at] = (p * (dp - inner)).astype(BF)
        dv[:n, :] += mm(probs[:n, :], g_heads[block])
        dk[:n, :] += mm(grads[:n, :], q_heads[...])
        dq = jnp.zeros((256, 256), F32)
        for head in range(4):
            dq = dq + mm_tn(grads[:n, 256 * head : 256 * head + 256], k_heads[head, :n, :])
        out[rows, 0:256] = unrotate(dq.astype(BF), rows)
    for block in range(4):
        rows = slice(256 * block, 256 * block + 256)
        out[rows, 256:512] = unrotate(dk[rows, :].astype(BF), rows)
        out[rows, 512:768] = dv[rows, :].astype(BF)


def attend_back(info, q, k, v, parts, log_total, cosine, sine):
    return call(
        attend_back_kernel,
        [((1024, 768), BF)],
        [
            ((1024, 256), BF),
            ((4, 1024, 256), BF),
            ((4, 1024, 256), BF),
            ((1024, 1024), BF),
            ((1024, 1024), BF),
            ((1024, 256), F32),
            ((1024, 256), F32),
        ],
        (info, q, k, v, *parts, log_total, cosine, sine),
        20,
    )[0]


def output_kernel(info, parts, w0, w1, w2, w3, a_o, keep, send, w, mix):
    z_at, x_at = info[7], info[8]
    for dy, piece in enumerate((w0, w1, w2, w3)):
        chip = (info[0] + dy) % 4
        mix[:, 256 * dy : 256 * dy + 256] = parts[dy]
        for dz in range(4):
            for dx in range(4):
                f = ((z_at + dz) % 4) * 4 + (x_at + dx) % 4
                rows = aligned(f * 64 + 16 * chip, 16)
                for part in range(8):
                    w[rows, 256 * part : 256 * part + 256] = piece[dz, dx, 16 * part : 16 * part + 16]
    keep[:, :WIDTH] = mm(mix[:ROWS, :], w[...])
    keep[:, WIDTH:] = mm(mix[:ROWS, :], a_o[...])
    send[:, :WIDTH] = mm(mix[ROWS:, :], w[...]).astype(BF)
    send[:, WIDTH:] = mm(mix[ROWS:, :], a_o[...]).astype(BF)


def project_output(info, mixes, pieces, a_o):
    return call(
        output_kernel,
        [((ROWS, 2176), F32), ((ROWS, 2176), BF), ((1024, WIDTH), BF)],
        [((256, 1024), BF)],
        (info, mixes, *pieces, a_o),
        8,
    )


def middle_kernel(info, keep, got, x, b_o, gain, resid, n2, low):
    summed = keep[...] + got[...].astype(F32)
    mask = lane_mask(info, (2 * info[0] + info[1]) * ROWS, ROWS)
    low_o = jnp.where(mask, summed[:, WIDTH:], 0.0).astype(BF)
    low[...] = low_o
    values = x[...].astype(F32) + summed[:, :WIDTH] + mm_nt(low_o, b_o[...])
    resid[...] = values
    inverse = lax.rsqrt(jnp.mean(values * values, -1, keepdims=True) + NORM_EPS)
    n2[...] = (values * inverse * gain[1:2, :]).astype(BF)


def middle(deps, info, keep, got, x, b_o, gain):
    return call(
        middle_kernel,
        [((ROWS, WIDTH), F32), ((ROWS, WIDTH), BF), ((ROWS, 128), BF)],
        [],
        (info, keep, got, x, b_o, gain),
        10,
        deps,
    )


def feed_kernel(
    step, info, n_near, n_far, g_near, g_far, w_g, w_u, w_d, a_gu, b_d, ff,
    keep_down, send_down, keep_back, send_back, hidden, grad_gate, grad_up, lows, n_rows, g_rows,
):
    chip = (info[0] + step) % 4
    n_rows[:ROWS] = n_near[chip]
    n_rows[ROWS:] = n_far[chip]
    g_rows[:ROWS] = g_near[chip]
    g_rows[ROWS:] = g_far[chip]
    mask = chip_mask(info, step)
    twice = jnp.concatenate([mask, mask], 1)
    low = jnp.where(twice, mm(n_rows[...], a_gu[...]), 0.0).astype(BF)
    glow = jnp.where(mask, mm(g_rows[...], b_d[...]), 0.0).astype(BF)
    lows[:, :256] = low
    lows[:, 256:384] = glow
    for block in range(4):
        at = slice(256 * block, 256 * block + 256)
        gate = mm(n_rows[...], w_g[:, at]) + mm_nt(low[:, :128], ff[at, 128:256])
        up = mm(n_rows[...], w_u[:, at]) + mm_nt(low[:, 128:], ff[at, 256:])
        grad_hidden = mm_nt(g_rows[...], w_d[at, :]) + mm_nt(glow, ff[at, :128])
        sig = 1.0 / (1.0 + jnp.exp(-gate))
        act = gate * sig
        hidden[:, at] = (act * up).astype(BF)
        grad_gate[:, at] = (grad_hidden * up * sig * (1.0 + gate * (1.0 - sig))).astype(BF)
        grad_up[:, at] = (grad_hidden * act).astype(BF)

    def put(keep, send, at, values):
        keep[:, at] = values[:ROWS]
        send[:, at] = values[ROWS:].astype(BF)

    for block in range(8):
        at = slice(256 * block, 256 * block + 256)
        put(keep_back, send_back, at, mm_nt(grad_gate[...], w_g[at, :]) + mm_nt(grad_up[...], w_u[at, :]))
        put(keep_down, send_down, at, mm(hidden[...], w_d[:, at]))
    glow_g = mm(grad_gate[...], ff[:, 128:256])
    glow_u = mm(grad_up[...], ff[:, 256:])
    low_d = mm(hidden[...], ff[:, :128])
    put(keep_back, send_back, slice(WIDTH, WIDTH + 128), glow_g)
    put(keep_back, send_back, slice(WIDTH + 128, WIDTH + 256), glow_u)
    put(keep_down, send_down, slice(WIDTH, WIDTH + 128), low_d)
    lows[:, 384:512] = jnp.where(mask, glow_g, 0.0).astype(BF)
    lows[:, 512:640] = jnp.where(mask, glow_u, 0.0).astype(BF)
    lows[:, 640:] = jnp.where(mask, low_d, 0.0).astype(BF)


def feed(step, deps, info, n_near, n_far, g_near, g_far, *weights):
    return call(
        functools.partial(feed_kernel, step),
        [
            ((ROWS, 2176), F32),
            ((ROWS, 2176), BF),
            ((ROWS, 2304), F32),
            ((ROWS, 2304), BF),
            ((256, 1024), BF),
            ((256, 1024), BF),
            ((256, 1024), BF),
            ((256, 768), BF),
        ],
        [((256, WIDTH), BF), ((256, WIDTH), BF)],
        (info, n_near, n_far, g_near, g_far, *weights),
        14,
        deps,
    )


def early_kernel(info, n_near, n_far, g_near, g_far, *refs):
    chunks, by_token, by_hidden = [refs[4 * i : 4 * i + 4] for i in range(4)], refs[-2], refs[-1]
    flip = lambda values: values.astype(F32).T.astype(BF)
    thins = [flip(chunk[3][...]) for chunk in chunks]
    rows = lambda i, j: thins[i][128 * j : 128 * j + 128]
    for j, (row, name) in enumerate(((2, 0), (0, 1), (1, 2))):
        total = sum(mm(rows(i, row), chunks[i][name][...]) for i in range(4))
        by_hidden[:, 128 * j : 128 * j + 128] = total.T.astype(BF)
    for j, (row, near, far) in enumerate(((3, n_near, n_far), (4, n_near, n_far), (5, g_near, g_far))):
        total = 0.0
        for i, d in enumerate(ORDER):
            chip = (info[0] + d) % 4
            total = total + mm(rows(i, row)[:, :ROWS], near[chip]) + mm(rows(i, row)[:, ROWS:], far[chip])
        by_token[:, 128 * j : 128 * j + 128] = total.T.astype(BF)


def early_sums(tokens, chunks, deps):
    args = [(), *tokens] + [part for chunk in chunks for part in chunk]
    return call(
        early_kernel, [((WIDTH, 384), BF), ((1024, 384), BF)], [], args, 8, deps
    )


def between_kernel(info, own, r1, r2, r3, a_gu, resid, og, gain, grad_resid, grad_attn):
    total = own[...] + r1[...].astype(F32) + r2[...].astype(F32) + r3[...].astype(F32)
    mask = lane_mask(info, (2 * info[0] + info[1]) * ROWS, ROWS)
    glow = jnp.where(jnp.concatenate([mask, mask], 1), total[:, WIDTH:], 0.0).astype(BF)
    grad = total[:, :WIDTH] + mm_nt(glow, a_gu[...])
    values = resid[...]
    inverse = lax.rsqrt(jnp.mean(values * values, -1, keepdims=True) + NORM_EPS)
    result = og[...].astype(F32) + norm_back(grad, values, inverse, gain[1:2, :])
    grad_resid[...] = result
    grad_attn[...] = result.astype(BF)


def between(deps, info, own, r1, r2, r3, a_gu, resid, og, gain):
    return call(
        between_kernel,
        [((ROWS, WIDTH), F32), ((ROWS, WIDTH), BF)],
        [],
        (info, own, r1, r2, r3, a_gu, resid, og, gain),
        10,
        deps,
    )


def combine_kernel(info, by_token, by_hidden, out):
    for f in range(16):
        out[f, :ROWS, :] = by_token[f * ROWS : f * ROWS + ROWS, :]
        out[f, ROWS:, :] = by_hidden[64 * f : 64 * f + 64, :]


def combine(by_token, by_hidden):
    return call(combine_kernel, [((16, 192, 384), BF)], [], ((), by_token, by_hidden), 8)[0]


def down_kernel(info, k0, k1, k2, k3, got, own, *outs):
    for i, (d, keep) in enumerate(zip(ORDER, (k0, k1, k2, k3))):
        total = keep[...] + got[i].astype(F32)
        if d:
            outs[d - 1][...] = total.astype(BF)
        else:
            own[...] = total


def down_pair(deps, kept, got):
    return call(
        down_kernel,
        [((ROWS, 2176), F32)] + [((ROWS, 2176), BF)] * 3,
        [],
        ((), *kept, got),
        8,
        deps,
    )


def result_kernel(info, own, r1, r2, r3, resid, b_d, out):
    total = own[...] + r1[...].astype(F32) + r2[...].astype(F32) + r3[...].astype(F32)
    mask = lane_mask(info, (2 * info[0] + info[1]) * ROWS, ROWS)
    low = jnp.where(mask, total[:, WIDTH:], 0.0).astype(BF)
    out[...] = (resid[...] + total[:, :WIDTH] + mm_nt(low, b_d[...])).astype(BF)


def result(info, own, r1, r2, r3, resid, b_d):
    return call(
        result_kernel, [((ROWS, WIDTH), BF)], [], (info, own, r1, r2, r3, resid, b_d), 10
    )[0]


def output_back_kernel(info, own, other, low_own, low_other, b_o, w_o, a_o, p0, p1, p2, p3, half, grad, mix):
    grad[:ROWS] = own[...]
    grad[ROWS:] = other[...]
    glow = jnp.where(chip_mask(info, 0), mm(grad[...], b_o[...]), 0.0).astype(BF)
    for chip in range(4):
        at = slice(256 * chip, 256 * chip + 256)
        mix[:, at] = (mm_nt(grad[...], w_o[at, :]) + mm_nt(glow, a_o[at, :])).astype(BF)
    for d, part in enumerate((p0, p1, p2, p3)):
        part[:, :256] = mix[:, aligned(256 * ((info[0] + d) % 4), 256)]
        part[:, 256:] = glow
    flip = lambda values: values.astype(F32).T.astype(BF)
    total = (mm(flip(low_own[...]), grad[:ROWS]) + mm(flip(low_other[...]), grad[ROWS:])).T.astype(BF)
    for f in range(16):
        rows = total[f * ROWS : f * ROWS + ROWS]
        half[64 * f : 64 * f + 64, :] = jnp.where(info[1] == 0, rows[:64], rows[64:])


def output_back(info, own, other, low_own, low_other, b_o, w_o, a_o):
    return call(
        output_back_kernel,
        [((256, 384), BF)] * 4 + [((1024, 128), BF)],
        [((256, WIDTH), BF), ((256, 1024), BF)],
        (info, own, other, low_own, low_other, b_o, w_o, a_o),
        8,
    )


def pick_rows(info, g, core, out):
    for d in range(4):
        chip = (info[0] + d) % 4
        out[d * ROWS : d * ROWS + ROWS, :] = g[aligned(256 * chip + ROWS * core, ROWS), :]


def input_send_kernel(info, g, w, send, rows):
    pick_rows(info, g, 1 - info[1], rows)
    for block in range(8):
        at = slice(256 * block, 256 * block + 256)
        send[:, at] = mm_nt(rows[...], w[at, :]).astype(BF)


def input_send(info, g, w):
    return call(input_send_kernel, [((512, WIDTH), BF)], [((512, 768), BF)], (info, g, w), 8)[0]


def input_pair_kernel(info, g, w, got, own, p1, p2, p3, rows):
    pick_rows(info, g, info[1], rows)
    for block in range(8):
        at = slice(256 * block, 256 * block + 256)
        total = mm_nt(rows[...], w[at, :]) + got[:, at].astype(F32)
        own[:, at] = total[:ROWS]
        for d, out in enumerate((p1, p2, p3)):
            out[:, at] = total[ROWS * (d + 1) : ROWS * (d + 2)].astype(BF)


def input_pair(deps, info, g, w, got):
    return call(
        input_pair_kernel,
        [((ROWS, WIDTH), F32)] + [((ROWS, WIDTH), BF)] * 3,
        [((512, 768), BF)],
        (info, g, w, got),
        8,
        deps,
    )


def squeeze(rows):
    i = lax.broadcasted_iota(jnp.int32, rows, 0) % ADAPTER_RANK
    j = lax.broadcasted_iota(jnp.int32, rows, 1) % ADAPTER_RANK
    return (i == j).astype(BF)


def narrow_kernel(info, g, b_q, b_k, b_v, low, mix, o0, o1, o2, o3, narrow, own):
    mask = lane_mask(info, 0, 1024)
    fold = squeeze((16, 128))
    flip = lambda values: values.astype(F32).T.astype(BF)
    for j, b in enumerate((b_q, b_k, b_v)):
        term = jnp.where(mask, mm(g[:, 256 * j : 256 * j + 256], b[...]), 0.0).astype(BF)
        narrow[16 * j : 16 * j + 16, :] = mm_nt(fold, term).astype(BF)
    low_t = flip(low[...])
    for j in range(3):
        total = mm(low_t[128 * j : 128 * j + 128], g[:, 256 * j : 256 * j + 256]).T.astype(BF)
        lanes = slice(128 * (j + 1), 128 * (j + 2))
        for head in range(4):
            if j == 2:
                own[head, :, lanes] = total[64 * head : 64 * head + 64]
            else:
                own[head, :32, lanes] = total[32 * head : 32 * head + 32]
                own[head, 32:, lanes] = total[128 + 32 * head : 160 + 32 * head]
    total = sum(
        mm(flip(part[:, 256:]), mix[aligned(256 * ((info[0] - d + 4) % 4), 256), :])
        for d, part in enumerate((o0, o1, o2, o3))
    ).T.astype(BF)
    for head in range(4):
        own[head, :, :128] = total[64 * head : 64 * head + 64]


def narrow_sums(deps, info, g, b_q, b_k, b_v, low, mix, parts):
    return call(
        narrow_kernel,
        [((48, 1024), BF), ((4, 64, 512), BF)],
        [],
        (info, g, b_q, b_k, b_v, low, mix, *parts),
        10,
        deps,
    )


def late_kernel(info, n0, n1, n2, n3, rows, out, glow_own):
    total = n0[...].astype(F32) + n1[...].astype(F32) + n2[...].astype(F32) + n3[...].astype(F32)
    total = total.astype(BF)
    s_at = 2 * info[0] + info[1]
    mask = lane_mask(info, 0, 1024)
    spread = squeeze((16, 128))
    wide = []
    for j in range(3):
        term = jnp.where(mask, mm_tn(total[16 * j : 16 * j + 16], spread), 0.0)
        wide.append(term)
    mask_own = lane_mask(info, s_at * ROWS, ROWS)
    for j in range(3):
        piece = jnp.zeros((ROWS, 128), F32)
        for block in range(8):
            piece = jnp.where(s_at == block, wide[j][block * ROWS : block * ROWS + ROWS], piece)
        glow_own[:, 128 * j : 128 * j + 128] = jnp.where(mask_own, piece, 0.0).astype(BF)
    thin = jnp.concatenate([term.T.astype(BF) for term in wide], 0)
    for f in range(8):
        at = slice(256 * f, 256 * f + 256)
        total = mm(thin, rows[:, at]).T
        for second in range(2):
            piece = jnp.zeros((16, 384), F32)
            for s in range(8):
                first = second * ROWS + 16 * s
                piece = jnp.where(s_at == s, total[first : first + 16], piece)
            out[2 * f + second] = piece.astype(BF)


def late_sums(deps, info, parts, rows):
    return call(
        late_kernel,
        [((16, 16, 384), BF), ((ROWS, 384), BF)],
        [],
        (info, *parts, rows),
        10,
        deps,
    )


def groups_kernel(info, values, out):
    total = values[0].astype(F32)
    for f in range(1, 16):
        total = total + values[f].astype(F32)
    out[...] = total.astype(BF)


def sum_groups(deps, values):
    return call(groups_kernel, [(values.shape[1:], BF)], [], ((), values), 8, deps)[0]


def last_kernel(info, own, r1, r2, r3, glow, a, resid_grad, x, gain, out):
    grad = own[...] + r1[...].astype(F32) + r2[...].astype(F32) + r3[...].astype(F32) + mm_nt(glow[...], a[...])
    values = x[...].astype(F32)
    inverse = lax.rsqrt(jnp.mean(values * values, -1, keepdims=True) + NORM_EPS)
    out[...] = resid_grad[...] + norm_back(grad, values, inverse, gain[0:1, :])


def last(info, own, r1, r2, r3, glow, a, resid_grad, x, gain):
    return call(
        last_kernel,
        [((ROWS, WIDTH), F32)],
        [],
        (info, own, r1, r2, r3, glow, a, resid_grad, x, gain),
        10,
    )[0]


def rms_inverse(values):
    return lax.rsqrt(jnp.mean(values * values, -1, keepdims=True) + NORM_EPS)


def norm_back(grad_norm, values, inverse, gain):
    normed = values * inverse
    scaled = grad_norm * gain
    return inverse * (scaled - normed * jnp.mean(scaled * normed, -1, keepdims=True))


def body(
    layer_input,
    output_gradient,
    norm_gain_pair,
    query_key_value_weight,
    output_weight,
    gate_up_weight,
    down_weight,
    adapter_input_model,
    adapter_output_model,
    adapter_input_hidden,
    adapter_output_hidden,
    spans,
    adapter_choice_rows,
):
    f_at, s_at = lax.axis_index("fs"), lax.axis_index("sp")
    y_at, c_at = s_at >> 1, s_at & 1
    z_at = f_at >> 2
    x_l = layer_input[0]
    og_l = output_gradient[0]
    rows = x_l.shape[0]
    tokens = 8 * rows
    gains = norm_gain_pair
    info = (spans, adapter_choice_rows)

    w_pack, ab_pack = pack(
        query_key_value_weight.transpose(1, 0, 2), adapter_input_model, adapter_output_model, output_weight
    )
    w_line, ab_line = line(w_pack, shift_x), line(ab_pack, shift_z)
    w_line, ab_line = stack_rows((), w_line, ab_line)
    w_parts, ab_parts = line(w_line, shift_z), line(ab_line, shift_x)
    n1_l = norm_first((w_pack,), info, x_l, gains)
    near = gather_y(n1_l)
    far = swap(near)
    g_near = gather_y(og_l)
    g_far = swap(g_near)
    feed_pack = pack_feed(
        (*w_parts[1:], *ab_parts[1:]),
        gate_up_weight,
        down_weight,
        adapter_input_model,
        adapter_output_model,
        adapter_input_hidden,
        adapter_output_hidden,
    )
    feed_all = lax.all_gather(feed_pack, "fs", axis=0, tiled=False)
    w_g = feed_all[:, :ROWS, :1024].reshape(WIDTH, 1024)
    w_u = feed_all[:, :ROWS, 1024:2048].reshape(WIDTH, 1024)
    a_gu = feed_all[:, :ROWS, 2048:2304].reshape(WIDTH, 256)
    b_d = feed_all[:, :ROWS, 2304:].reshape(WIDTH, 128)
    w_d = feed_all[:, ROWS:, :2048].reshape(1024, WIDTH)
    ff = feed_all[:, ROWS:, 2048:].reshape(1024, 384)

    at = jnp.arange(tokens, dtype=jnp.int32)
    position = at - jnp.where(at >= spans[0, 0] + spans[0, 1], spans[0, 1], 0)
    freq = ROPE_BASE ** (-(jnp.arange(32, dtype=F32) * 2.0 / HEAD_SIZE))
    phase = position.astype(F32)[:, None] * jnp.tile(freq, 4)[None, :]
    cosine, sine = jnp.cos(phase), jnp.sin(phase)

    o_parts = line(stack_output(tuple(ab_parts[1:]), w_parts), shift)
    q, k, v, low_qkv, n1, w_qkv, a_qkv, b_q, b_k, b_v, a_o, b_o = project_qkv(
        (), info, w_parts, ab_parts, near, far, cosine, sine
    )
    mix, log_total = attend(info, q, k, v)
    mixes = exchange_y(mix.reshape(4, 256, 256))
    keep, send, w_o = project_output(info, mixes, o_parts, a_o)
    resid, n2_l, low_o = middle((), info, keep, swap(send), x_l, b_o, gains)

    n_near = order_chips(line(n2_l, shift))
    token_rows = (n_near, swap(n_near), g_near, g_far)
    chunks, kept, sent, back, got = [], [], [], {}, []
    for d in ORDER:
        deps = [chunks[-1][-1]] if chunks else []
        deps += got[-2:-1]
        keep_down, send_down, keep_back, send_back, *chunk = feed(
            d, deps, info, *token_rows, w_g, w_u, w_d, a_gu, b_d, ff
        )
        chunks.append(chunk)
        kept.append(keep_down)
        sent.append(send_down)
        got.append(swap(send_back))
        pair = keep_back + got[-1].astype(F32)
        back[d] = shift(pair.astype(BF), d if d < 3 else -1) if d else pair
    by_token, by_hidden = early_sums(token_rows, chunks, [got[-1]])
    early = combine(by_token, by_hidden)
    low_other = swap(low_o)
    early = lax.all_to_all(early, "fs", split_axis=0, concat_axis=0, tiled=False)
    grad_resid, grad_attn = between((by_token,), info, back[0], back[1], back[2], back[3], a_gu, resid, og_l, gains)

    *parts, half_o = output_back(info, grad_attn, swap(grad_attn), low_o, low_other, b_o, w_o, a_o)
    parts = [parts[0]] + [shift(parts[d], d) for d in (1, 2, 3)]
    g_all = attend_back(info, q, k, v, parts, log_total, cosine, sine)
    send = input_send(info, g_all, w_qkv)
    narrow, own = narrow_sums((send,), info, g_all, b_q, b_k, b_v, low_qkv, mix, parts)
    pair, *total = input_pair((narrow,), info, g_all, w_qkv, swap(send))
    total = [shift(total[d - 1], d if d < 3 else -1) for d in (1, 2, 3)]
    narrow = (narrow.astype(F32) + swap(narrow).astype(F32)).astype(BF)
    late, glow_own = late_sums((pair, early), info, line(narrow, shift), n1)
    grad_in = last(info, pair, *total, glow_own, a_qkv, grad_resid, x_l, gains)
    down = down_pair(tuple(total), kept, swap(stack_rows((g_all,), sent)[0]))
    layer_output = result(
        info, down[0], *[shift(down[d], d if d < 3 else -1) for d in (1, 2, 3)], resid, b_d
    )

    def to_all(values):
        mine = jnp.stack(line(values, shift))
        other = swap(mine)
        both = jnp.stack([jnp.where(c_at == 0, mine, other), jnp.where(c_at == 0, other, mine)], 1)
        both = lax.dynamic_slice_in_dim(jnp.concatenate([both, both], 0), (4 - y_at) & 3, 4, 0)
        return both.astype(F32)

    early = to_all(sum_groups((late,), early))
    spread = jnp.sum(early[:, :, :128], (0, 1)).reshape(128, 3, 128).transpose(1, 0, 2)
    fed = early[:, :, 128:].reshape(512, 3, 128).transpose(1, 0, 2)
    own = lax.dynamic_update_slice(jnp.zeros((16, 16, 2048), BF), own.reshape(4, 16, 2048), (4 * y_at, 0, 0))
    final = jnp.concatenate([late, own, half_o.reshape(16, 16, 512)], 2)
    final = lax.all_to_all(final, "fs", split_axis=0, concat_axis=0, tiled=False)
    final = to_all(sum_groups(total, final))
    first = final[..., :384].reshape(128, 3, 128).transpose(1, 0, 2)
    own = lax.dynamic_index_in_dim(final[..., 384:2432], z_at, 0, False).reshape(128, 4, 128).transpose(1, 0, 2)
    b_o_grad = jnp.sum(final[..., 2432:], 0).reshape(1, 128, 128)
    grad_in_d = jnp.concatenate([first, own[:1], spread[:2]], 0)
    grad_out_d = jnp.concatenate([own[1:], b_o_grad, spread[2:]], 0)
    return (layer_output[None], grad_in[None], grad_in_d, grad_out_d, fed[:1], fed[1:])


def solution(mesh):
    in_specs = (
        P("fs", "sp", None),
        P("fs", "sp", None),
        P(),
        P("fs", None, None),
        P("fs", None),
        P("fs", None, None),
        P("fs", None),
        P(None, "fs", None),
        P(None, "fs", None),
        P(None, "fs", None),
        P(None, "fs", None),
        P("fs", None),
        P("fs", None),
    )
    out_specs = (
        P("fs", "sp", None),
        P("fs", "sp", None),
        P(None, "fs", None),
        P(None, "fs", None),
        P(None, "fs", None),
        P(None, "fs", None),
    )
    return jax.shard_map(body, mesh=mesh, in_specs=in_specs, out_specs=out_specs, check_vma=False)
```

time: 708 us -> 468 us (0.66)
  matrix products: 147 us -> 0 us
  Pallas kernels: 0 us -> 125 us
  waiting for transfers between devices: 233 us -> 123 us
  other arithmetic: 115 us -> 10.9 us
  starting transfers between devices: 45.9 us -> 82.5 us
  blocking collectives: 35.6 us -> 0 us
    dot_general x52 -> x0, matrix products: 147 us -> none  [the longest x20 50.2 us: mm(): return jnp.dot(left, right, preferred_element_type=F32)]
    pallas_call x0 -> x29, Pallas kernels: none -> 125 us  [call(): pl.pallas_call(run, out_shape=outs, in_specs=[SMEM] * first + [VMEM] * le...]
    all_gather x4 -> x3, waiting for transfers between devices: 74.8 us -> 0.04 us  [the longest x2 0.02 us: gather_y(): lax.all_gather(x, 'sp', axis=0, tiled=False, axis_index_groups=Y_LINES)]
    ppermute x24 -> x27, waiting for transfers between devices: 125 us -> 66.9 us  [shift(): lax.ppermute(x, 'sp', [(i, (i // 2 + chips) % 4 * 2 + i % 2) for i in ran...]
    unnamed x237 -> x275, local copies, waits for them, and re-layouts: 25.4 us -> 80 us
    ppermute x0 -> x12, waiting for transfers between devices: none -> 42.4 us  [the longest x6 29.6 us: shift_x(): lax.ppermute(x, 'fs', [(i, i - i % 4 + (i + chips) % 4) for i in range(16)])]
    all_to_all x1 -> x0, blocking collectives: 35.6 us -> none  [body(): lax.all_to_all(everything, 'fs', split_axis=0, concat_axis=0, tiled=False)]
    ppermute x0 -> x12, starting transfers between devices: none -> 23.8 us  [the longest x6 12.5 us: shift_z(): return lax.ppermute(x, 'fs', [(i, (i + 4 * chips) % 16) for i in range(16)])]
  transfers between devices with their start and end apart: 37 -> 60, of which waited for: 20 -> 15; matrix products, arithmetic and copies ran while one was open for 36% -> 7% of each run, Pallas kernels for 0% -> 23%
where the time goes in v2:
time: 468 us; the launch traced here: 460 us
  Pallas kernels  125 us (27%)
  waiting for transfers between devices  123 us (26%)
  local copies, waits for them, and re-layouts  103 us (22%)
  starting transfers between devices  82.5 us (18%)
  between operations  16.6 us (4%)
  other arithmetic  10.9 us (2%)
    pallas_call x29, Pallas kernels, call(): pl.pallas_call(run, out_shape=outs, in_specs=[SMEM] * first + [VMEM] * le...  125 us
    unnamed x275, local copies, waits for them, and re-layouts  80 us
    ppermute x27, waiting for transfers between devices, shift(): lax.ppermute(x, 'sp', [(i, (i // 2 + chips) % 4 * 2 + i % 2) for i in ran...  66.9 us
    ppermute x27, starting transfers between devices, shift(): lax.ppermute(x, 'sp', [(i, (i // 2 + chips) % 4 * 2 + i % 2) for i in ran...  37.6 us
    ppermute x6, waiting for transfers between devices, shift_x(): lax.ppermute(x, 'fs', [(i, i - i % 4 + (i + chips) % 4) for i in range(16)])  29.6 us
    ppermute x6, waiting for transfers between devices, shift_z(): return lax.ppermute(x, 'fs', [(i, (i + 4 * chips) % 16) for i in range(16)])  12.8 us
    ppermute x6, starting transfers between devices, shift_z(): return lax.ppermute(x, 'fs', [(i, (i + 4 * chips) % 16) for i in range(16)])  12.5 us
    ppermute x6, starting transfers between devices, shift_x(): lax.ppermute(x, 'fs', [(i, i - i % 4 + (i + chips) % 4) for i in range(16)])  11.3 us
  transfers between devices with their start and end apart: 60, of which 15 were waited for; matrix products, arithmetic and copies ran while one was open for 7% of the time, Pallas kernels for 23%

profile of v2, /device:TPU:0, one launch (start us, length us, event | category | flops | bytes accessed | tf_op | source)
XLA Modules:
  0.0 460.4 jit_solution(13109163107749715560)
XLA Ops:
  22.4 3.6 collective-permute-start.4
  29.8 3.7 collective-permute-done.3.refs_5_
  43.4 9.2 %collective-permute-done.11.refs_9_.refs_6_.refs_11_ = bf16[4,128,768]{2,1,0:T(8,128)(2,1)S(1)} collective-permute-done((bf16[4,128,768]{2,1,0:T(8,128)(2,1)S(1)}, bf16[4,128,768]{2,1,0:T(8,128)(2,1)S(1)}, u32[]{:S(2)}, u32[]{:S(2)}) %collective-permute-start.11) | collective-permute-done | bytes 786464 | tf_op jit(solution)/shard_map/ppermute | solution.py:47
  56.1 14.5 %collective-permute-done.10.refs_8_.refs_5_.refs_10_ = bf16[4,128,768]{2,1,0:T(8,128)(2,1)S(1)} collective-permute-done((bf16[4,128,768]{2,1,0:T(8,128)(2,1)S(1)}, bf16[4,128,768]{2,1,0:T(8,128)(2,1)S(1)}, u32[]{:S(2)}, u32[]{:S(2)}) %collective-permute-start.10) | collective-permute-done | bytes 786464 | tf_op jit(solution)/shard_map/ppermute | solution.py:47
  70.6 5.9 %collective-permute-done.9.refs_7_.refs_4_.refs_9_ = bf16[4,128,768]{2,1,0:T(8,128)(2,1)S(1)} collective-permute-done((bf16[4,128,768]{2,1,0:T(8,128)(2,1)S(1)}, bf16[4,128,768]{2,1,0:T(8,128)(2,1)S(1)}, u32[]{:S(2)}, u32[]{:S(2)}) %collective-permute-start.9) | collective-permute-done | bytes 786464 | tf_op jit(solution)/shard_map/ppermute | solution.py:47
  76.5 6.3 %collective-permute-done.7.refs_4_.refs_2_.refs_7_ = bf16[4,128,1024]{2,1,0:T(8,128)(2,1)S(1)} collective-permute-done((bf16[4,128,1024]{2,1,0:T(8,128)(2,1)S(1)}, bf16[4,128,1024]{2,1,0:T(8,128)(2,1)S(1)}, u32[]{:S(2)}, u32[]{:S(2)}) %collective-permute-start.7) | collective-permute-done | bytes 1048608 | tf_op jit(solution)/shard_map/ppermute | solution.py:43
  88.5 3.0 shard_map.181
  102.5 3.0 collective-permute-start.14
  118.3 8.5 %shard_map.175 = (bf16[1024,256]{1,0:T(8,128)(2,1)S(1)}, bf16[1024,256]{1,0:T(8,128)(2,1)S(1)}, bf16[1024,256]{1,0:T(8,128)(2,1)S(1)}, bf16[1024,384]{1,0:T(8,12...) custom-call(s32[1,3]{1,0:T(1,128)S(1)} %copy-done.99, ...), custom_call_target="tpu_custom_call" | custom-call | flops 1024 | bytes 1024 | tf_op jit(solution)/shard_map/pallas_call | solution.py:93
  133.4 16.6 %shard_map.176 = (bf16[1024,256]{1,0:T(8,128)(2,1)}, f32[8,1024]{1,0:T(8,128)S(1)}) custom-call(s32[1,3]{1,0:T(1,128)S(1)} %copy-done.99, s32[1,3]{1,0:T(1,128)S(1)} %copy-done.102, bf16[1024,256]{1,0:T(8,128)(2,1)S(1)} %get-tuple-element.87.refs_2_, bf16[1024,256]{1,0:T(8,128)(2,1)S(1)} %get-tuple-element.88.refs_3_, ...), custom_call_target="tpu_custom_call" | custom-call | flops 1024 | bytes 1024 | tf_op jit(solution)/shard_map/pallas_call | solution.py:93
  150.8 3.5 all-to-all-start
  154.4 9.6 %all-to-all-done.refs_2_ = bf16[4,256,256]{2,1,0:T(8,128)(2,1)S(1)} async-done(((bf16[4,256,256]{2,1,0:T(8,128)(2,1)}), bf16[4,256,256]{2,1,0:T(8,128)(2,1)S(1)}, u32[]{:S(2)}, u32[]{:S(2)}) %all-to-all-start) | async-done | bytes 524320 | tf_op jit(solution)/shard_map/all_to_all | solution.py:58
  163.9 4.2 shard_map.178
  177.4 23.2 %collective-permute-done.19.refs_3_ = bf16[128,2048]{1,0:T(8,128)(2,1)S(1)} collective-permute-done((bf16[128,2048]{1,0:T(8,128)(2,1)S(1)}, bf16[128,2048]{1,0:T(8,128)(2,1)S(1)}, u32[]{:S(2)}, u32[]{:S(2)}) %collective-permute-start.19) | collective-permute-done | bytes 524320 | tf_op jit(solution)/shard_map/ppermute | solution.py:35
  212.6 4.1 fusion.8
  216.8 10.8 %shard_map.182 = (f32[128,2176]{1,0:T(8,128)S(1)}, bf16[128,2176]{1,0:T(8,128)(2,1)S(1)}, f32[128,2304]{1,0:T(8,128)S(1)}, bf16[128,2304]{1,0:T(8,128)(2,1)S(1)}...) custom-call(s32[1,3]{1,0:T(1,128)S(1)} %copy-done.99, ...), custom_call_target="tpu_custom_call" | custom-call | flops 1024 | bytes 1024 | tf_op jit(solution)/shard_map/pallas_call | solution.py:93
  229.3 10.8 %shard_map.183 = (f32[128,2176]{1,0:T(8,128)S(1)}, bf16[128,2176]{1,0:T(8,128)(2,1)S(1)}, f32[128,2304]{1,0:T(8,128)S(1)}, bf16[128,2304]{1,0:T(8,128)(2,1)S(1)}...) custom-call(s32[1,3]{1,0:T(1,128)S(1)} %copy-done.99, ...), custom_call_target="tpu_custom_call" | custom-call | flops 1024 | bytes 1024 | tf_op jit(solution)/shard_map/pallas_call | solution.py:93
  241.3 10.9 %shard_map.184 = (f32[128,2176]{1,0:T(8,128)S(1)}, bf16[128,2176]{1,0:T(8,128)(2,1)S(1)}, f32[128,2304]{1,0:T(8,128)S(1)}, bf16[128,2304]{1,0:T(8,128)(2,1)S(1)}...) custom-call(s32[1,3]{1,0:T(1,128)S(1)} %copy-done.99, ...), custom_call_target="tpu_custom_call" | custom-call | flops 1024 | bytes 1024 | tf_op jit(solution)/shard_map/pallas_call | solution.py:93
  254.6 10.9 %shard_map.185 = (f32[128,2176]{1,0:T(8,128)S(1)}, bf16[128,2176]{1,0:T(8,128)(2,1)S(1)}, f32[128,2304]{1,0:T(8,128)S(1)}, bf16[128,2304]{1,0:T(8,128)(2,1)S(1)}...) custom-call(s32[1,3]{1,0:T(1,128)S(1)} %copy-done.99, ...), custom_call_target="tpu_custom_call" | custom-call | flops 1024 | bytes 1024 | tf_op jit(solution)/shard_map/pallas_call | solution.py:93
  267.5 6.7 %shard_map.186 = (bf16[2048,384]{1,0:T(8,128)(2,1)S(1)}, bf16[1024,384]{1,0:T(8,128)(2,1)S(1)}) custom-call(bf16[4,128,2048]{2,1,0:T(8,128)(2,1)S(1)} %shard_map.180.refs_2_.refs_0_, bf16[4,128,2048]{2,1,0:T(8,128)(2,1)} %collective-permute-done.20.refs_3_.refs_1_, bf16[4,128,2048]{2,1,0:T(8,128)(2,1)S(1)} %copy-done, ...), custom_call_target="tpu_custom_call" | custom-call | flops 1024 | bytes 1024 | tf_op jit(solution)/shard_map/pallas_call | solution.py:93
  274.4 7.3 %collective-permute-done.28.refs_5_ = bf16[128,2304]{1,0:T(8,128)(2,1)S(1)} collective-permute-done((bf16[128,2304]{1,0:T(8,128)(2,1)S(1)}, bf16[128,2304]{1,0:T(8,128)(2,1)S(1)}, u32[]{:S(2)}, u32[]{:S(2)}) %collective-permute-start.28) | collective-permute-done | bytes 589856 | tf_op jit(solution)/shard_map/ppermute | solution.py:35
  296.2 7.5 %all-to-all-start.1 = ((bf16[16,192,384]{2,1,0:T(8,128)(2,1)}), bf16[16,192,384]{2,1,0:T(8,128)(2,1)}, u32[]{:S(2)}, u32[]{:S(2)}) async-start(bf16[16,192,384]{2,1,0:T(8,128)(2,1)} %shard_map.196), calls=%async_computation.1 | async-start | bytes 4718592 | tf_op jit(solution)/shard_map/all_to_all | solution.py:911
  312.2 8.8 %shard_map.189.refs_4_.refs_2_ = bf16[1024,768]{1,0:T(8,128)(2,1)S(1)} custom-call(s32[1,3]{1,0:T(1,128)S(1)} %copy-done.100, s32[1,3]{1,0:T(1,128)S(1)} %copy-done.103, bf16[1024,256]{1,0:T(8,128)(2,1)S(1)} %copy-done.44, bf16[1024,256]{1,0:T(8,128)(2,1)S(1)} %copy-done.46, bf16[1024,256]{1,0:T(8,128)(2,1)S(1)} %copy-done.48, ...), custom_call_target="tpu_custom_call" | custom-call | flops 1024 | bytes 1024 | tf_op jit(solution)/shard_map/pallas_call | solution.py:93
  321.1 3.7 shard_map.191.refs_12_
  343.3 3.4 shard_map.193
  357.0 7.3 %all-to-all-start.2 = ((bf16[16,16,2944]{2,1,0:T(8,128)(2,1)}), bf16[16,16,2944]{2,1,0:T(8,128)(2,1)S(1)}, u32[]{:S(2)}, u32[]{:S(2)}) async-start(bf16[16,16,2944]{2,1,0:T(8,128)(2,1)} %pad_maximum_fusion), calls=%async_computation.2 | async-start | bytes 3014656 | tf_op jit(solution)/shard_map/all_to_all | solution.py:941
  372.4 5.0 %collective-permute-done.52 = bf16[192,384]{1,0:T(8,128)(2,1)S(1)} collective-permute-done((bf16[192,384]{1,0:T(8,128)(2,1)S(1)}, bf16[192,384]{1,0:T(8,128)(2,1)S(1)}, u32[]{:S(2)}, u32[]{:S(2)}) %collective-permute-start.52) | collective-permute-done | bytes 147488 | tf_op jit(solution)/shard_map/ppermute | solution.py:35
  377.7 21.7 %collective-permute-done.50 = bf16[192,384]{1,0:T(8,128)(2,1)S(1)} collective-permute-done((bf16[192,384]{1,0:T(8,128)(2,1)S(1)}, bf16[192,384]{1,0:T(8,128)(2,1)S(1)}, u32[]{:S(2)}, u32[]{:S(2)}) %collective-permute-start.50) | collective-permute-done | bytes 147488 | tf_op jit(solution)/shard_map/ppermute | solution.py:35
  403.7 3.0 collective-permute-start.47
  413.0 3.1 shard_map.194
  437.2 6.6 %collective-permute-done.39.refs_3_ = bf16[128,2176]{1,0:T(8,128)(2,1)} collective-permute-done((bf16[128,2176]{1,0:T(8,128)(2,1)}, bf16[128,2176]{1,0:T(8,128)(2,1)}, u32[]{:S(2)}, u32[]{:S(2)}) %collective-permute-start.39) | collective-permute-done | bytes 557088 | tf_op jit(solution)/shard_map/ppermute | solution.py:35
  443.8 3.1 collective-permute-done.41.refs_5_
  (444 shorter events, 194.4 us)
Async XLA Ops:
  7.2 87.9 %all-gather.8.cloned.1.call-start = ((), (), s32[]{:S(2)}) async-start(), calls=%async_computation.4 | async-start | bytes 2621440 | tf_op jit(solution)/shard_map/all_gather | solution.py:54
  13.9 163.5 %all-gather.6.cloned.1.call-start = ((), (), s32[]{:S(2)}) async-start(), calls=%async_computation.3 | async-start | bytes 2621440 | tf_op jit(solution)/shard_map/all_gather | solution.py:54
  14.6 191.7 %all-gather.10.cloned.1.call-start = ((), (), s32[]{:S(2)}) async-start(), calls=%async_computation.5 | async-start | bytes 15876096 | tf_op jit(solution)/shard_map/all_gather | solution.py:870
  33.6 19.0 %collective-permute-start.11 = (bf16[4,128,768]{2,1,0:T(8,128)(2,1)S(1)}, bf16[4,128,768]{2,1,0:T(8,128)(2,1)S(1)}, u32[]{:S(2)}, u32[]{:S(2)}) collective-permute-start(bf16[4,128,768]{2,1,0:T(8,128)(2,1)S(1)} %get-tuple-element.86.refs_6_), channel_id=1, source_target_pairs={{0,8},{8,16},{16,24},{24,0},{32,40},{40,48},{48,56},{56,32},{64,72... | collective-permute-start | bytes 2359304 | tf_op jit(solution)/shard_map/ppermute | solution.py:47
  34.3 42.3 %collective-permute-start.8 = (bf16[4,128,1024]{2,1,0:T(8,128)(2,1)S(1)}, bf16[4,128,1024]{2,1,0:T(8,128)(2,1)S(1)}, u32[]{:S(2)}, u32[]{:S(2)}) collective-permute-start(bf16[4,128,1024]{2,1,0:T(8,128)(2,1)S(1)} %get-tuple-element.85.refs_2_.refs_0_), channel_id=1, source_target_pairs={{0,32},{8,40},{16,48},{24,56},{32,64},{40,72},{48,80},{56,88},{64,... | collective-permute-start | bytes 3145736 | tf_op jit(solution)/shard_map/ppermute | solution.py:43
  36.0 46.8 %collective-permute-start.7 = (bf16[4,128,1024]{2,1,0:T(8,128)(2,1)S(1)}, bf16[4,128,1024]{2,1,0:T(8,128)(2,1)S(1)}, u32[]{:S(2)}, u32[]{:S(2)}) collective-permute-start(bf16[4,128,1024]{2,1,0:T(8,128)(2,1)S(1)} %get-tuple-element.85.refs_2_.refs_0_), channel_id=1, source_target_pairs={{0,64},{8,72},{16,80},{24,88},{32,96},{40,104},{48,112},{56,120},{... | collective-permute-start | bytes 3145736 | tf_op jit(solution)/shard_map/ppermute | solution.py:43
  38.4 44.4 %collective-permute-start.6 = (bf16[4,128,1024]{2,1,0:T(8,128)(2,1)S(1)}, bf16[4,128,1024]{2,1,0:T(8,128)(2,1)S(1)}, u32[]{:S(2)}, u32[]{:S(2)}) collective-permute-start(bf16[4,128,1024]{2,1,0:T(8,128)(2,1)S(1)} %get-tuple-element.85.refs_2_.refs_0_), channel_id=1, source_target_pairs={{0,96},{8,104},{16,112},{24,120},{32,0},{40,8},{48,16},{56,24},{64... | collective-permute-start | bytes 3145736 | tf_op jit(solution)/shard_map/ppermute | solution.py:43
  41.0 29.6 %collective-permute-start.10 = (bf16[4,128,768]{2,1,0:T(8,128)(2,1)S(1)}, bf16[4,128,768]{2,1,0:T(8,128)(2,1)S(1)}, u32[]{:S(2)}, u32[]{:S(2)}) collective-permute-start(bf16[4,128,768]{2,1,0:T(8,128)(2,1)S(1)} %get-tuple-element.86.refs_6_), channel_id=1, source_target_pairs={{0,16},{8,24},{16,0},{24,8},{32,48},{40,56},{48,32},{56,40},{64,80... | collective-permute-start | bytes 2359304 | tf_op jit(solution)/shard_map/ppermute | solution.py:47
  52.6 23.9 %collective-permute-start.9 = (bf16[4,128,768]{2,1,0:T(8,128)(2,1)S(1)}, bf16[4,128,768]{2,1,0:T(8,128)(2,1)S(1)}, u32[]{:S(2)}, u32[]{:S(2)}) collective-permute-start(bf16[4,128,768]{2,1,0:T(8,128)(2,1)S(1)} %get-tuple-element.86.refs_6_), channel_id=1, source_target_pairs={{0,24},{8,0},{16,8},{24,16},{32,56},{40,32},{48,40},{56,48},{64,88... | collective-permute-start | bytes 2359304 | tf_op jit(solution)/shard_map/ppermute | solution.py:47
  101.0 53.4 %collective-permute-start.15 = (bf16[4,4,128,256]{3,2,1,0:T(8,128)(2,1)}, bf16[4,4,128,256]{3,2,1,0:T(8,128)(2,1)}, u32[]{:S(2)}, u32[]{:S(2)}) collective-permute-start(bf16[4,4,128,256]{3,2,1,0:T(8,128)(2,1)} %shard_map.177.refs_3_), channel_id=1, source_target_pairs={{0,2},{1,3},{2,4},{3,5},{4,6},{5,7},{6,0},{7,1},{8,10},{9,11},{10,... | collective-permute-start | bytes 3145736 | tf_op jit(solution)/shard_map/ppermute | solution.py:35
  102.5 51.9 %collective-permute-start.14 = (bf16[4,4,128,256]{3,2,1,0:T(8,128)(2,1)}, bf16[4,4,128,256]{3,2,1,0:T(8,128)(2,1)}, u32[]{:S(2)}, u32[]{:S(2)}) collective-permute-start(bf16[4,4,128,256]{3,2,1,0:T(8,128)(2,1)} %shard_map.177.refs_3_), channel_id=1, source_target_pairs={{0,4},{1,5},{2,6},{3,7},{4,0},{5,1},{6,2},{7,3},{8,12},{9,13},{10,... | collective-permute-start | bytes 3145736 | tf_op jit(solution)/shard_map/ppermute | solution.py:35
  105.5 48.9 %collective-permute-start.13 = (bf16[4,4,128,256]{3,2,1,0:T(8,128)(2,1)}, bf16[4,4,128,256]{3,2,1,0:T(8,128)(2,1)}, u32[]{:S(2)}, u32[]{:S(2)}) collective-permute-start(bf16[4,4,128,256]{3,2,1,0:T(8,128)(2,1)} %shard_map.177.refs_3_), channel_id=1, source_target_pairs={{0,6},{1,7},{2,0},{3,1},{4,2},{5,3},{6,4},{7,5},{8,14},{9,15},{10,... | collective-permute-start | bytes 3145736 | tf_op jit(solution)/shard_map/ppermute | solution.py:35
  174.1 26.4 %collective-permute-start.19 = (bf16[128,2048]{1,0:T(8,128)(2,1)S(1)}, bf16[128,2048]{1,0:T(8,128)(2,1)S(1)}, u32[]{:S(2)}, u32[]{:S(2)}) collective-permute-start(bf16[128,2048]{1,0:T(8,128)(2,1)S(1)} %get-tuple-element.95.refs_0_), channel_id=1, source_target_pairs={{0,2},{1,3},{2,4},{3,5},{4,6},{5,7},{6,0},{7,1},{8,10},{9,11},{10,... | collective-permute-start | bytes 1572872 | tf_op jit(solution)/shard_map/ppermute | solution.py:35
  174.6 26.8 %collective-permute-start.18 = (bf16[128,2048]{1,0:T(8,128)(2,1)S(1)}, bf16[128,2048]{1,0:T(8,128)(2,1)S(1)}, u32[]{:S(2)}, u32[]{:S(2)}) collective-permute-start(bf16[128,2048]{1,0:T(8,128)(2,1)S(1)} %get-tuple-element.95.refs_0_), channel_id=1, source_target_pairs={{0,4},{1,5},{2,6},{3,7},{4,0},{5,1},{6,2},{7,3},{8,12},{9,13},{10,... | collective-permute-start | bytes 1572872 | tf_op jit(solution)/shard_map/ppermute | solution.py:35
  176.6 25.6 %collective-permute-start.17 = (bf16[128,2048]{1,0:T(8,128)(2,1)S(1)}, bf16[128,2048]{1,0:T(8,128)(2,1)S(1)}, u32[]{:S(2)}, u32[]{:S(2)}) collective-permute-start(bf16[128,2048]{1,0:T(8,128)(2,1)S(1)} %get-tuple-element.95.refs_0_), channel_id=1, source_target_pairs={{0,6},{1,7},{2,0},{3,1},{4,2},{5,3},{6,4},{7,5},{8,14},{9,15},{10,... | collective-permute-start | bytes 1572872 | tf_op jit(solution)/shard_map/ppermute | solution.py:35
  177.4 39.4 %collective-permute-start.21 = (bf16[4,128,2048]{2,1,0:T(8,128)(2,1)}, bf16[4,128,2048]{2,1,0:T(8,128)(2,1)}, u32[]{:S(2)}, u32[]{:S(2)}) collective-permute-start(bf16[4,128,2048]{2,1,0:T(8,128)(2,1)} %all-gather.6.cloned.1.call-done.refs_4_.refs_2_), channel_id=1, source_target_pairs={{0,1},{1,0},{2,3},{3,2},{4,5},{5,4},{6,7},{7,6},{8,9},{9,8},{10,11... | collective-permute-start | bytes 6291464 | tf_op jit(solution)/shard_map/ppermute | solution.py:39
  240.4 34.0 %collective-permute-start.26 = (bf16[128,2304]{1,0:T(8,128)(2,1)S(1)}, bf16[128,2304]{1,0:T(8,128)(2,1)S(1)}, u32[]{:S(2)}, u32[]{:S(2)}) collective-permute-start(bf16[128,2304]{1,0:T(8,128)(2,1)S(1)} %add_convert_fusion.1), channel_id=1, source_target_pairs={{0,4},{1,5},{2,6},{3,7},{4,0},{5,1},{6,2},{7,3},{8,12},{9,13},{10,... | collective-permute-start | bytes 1769480 | tf_op jit(solution)/shard_map/ppermute | solution.py:35
  252.5 21.9 %collective-permute-start.25 = (bf16[128,2304]{1,0:T(8,128)(2,1)S(1)}, bf16[128,2304]{1,0:T(8,128)(2,1)S(1)}, u32[]{:S(2)}, u32[]{:S(2)}) collective-permute-start(bf16[128,2304]{1,0:T(8,128)(2,1)S(1)} %add_convert_fusion.2), channel_id=1, source_target_pairs={{0,2},{1,3},{2,4},{3,5},{4,6},{5,7},{6,0},{7,1},{8,10},{9,11},{10,... | collective-permute-start | bytes 1769480 | tf_op jit(solution)/shard_map/ppermute | solution.py:35
  296.2 53.6 %all-to-all-start.1 = ((bf16[16,192,384]{2,1,0:T(8,128)(2,1)}), bf16[16,192,384]{2,1,0:T(8,128)(2,1)}, u32[]{:S(2)}, u32[]{:S(2)}) async-start(bf16[16,192,384]{2,1,0:T(8,128)(2,1)} %shard_map.196), calls=%async_computation.1 | async-start | bytes 4718592 | tf_op jit(solution)/shard_map/all_to_all | solution.py:911
  335.5 71.5 %collective-permute-start.34 = (bf16[4,128,2176]{2,1,0:T(8,128)(2,1)}, bf16[4,128,2176]{2,1,0:T(8,128)(2,1)}, u32[]{:S(2)}, u32[]{:S(2)}) collective-permute-start(bf16[4,128,2176]{2,1,0:T(8,128)(2,1)} %copy-done.37), channel_id=1, source_target_pairs={{0,1},{1,0},{2,3},{3,2},{4,5},{5,4},{6,7},{7,6},{8,9},{9,8},{10,11... | collective-permute-start | bytes 6684680 | tf_op jit(solution)/shard_map/ppermute | solution.py:39
  357.0 44.2 %all-to-all-start.2 = ((bf16[16,16,2944]{2,1,0:T(8,128)(2,1)}), bf16[16,16,2944]{2,1,0:T(8,128)(2,1)S(1)}, u32[]{:S(2)}, u32[]{:S(2)}) async-start(bf16[16,16,2944]{2,1,0:T(8,128)(2,1)} %pad_maximum_fusion), calls=%async_computation.2 | async-start | bytes 3014656 | tf_op jit(solution)/shard_map/all_to_all | solution.py:941
  369.3 31.1 %collective-permute-start.36 = (bf16[128,2048]{1,0:T(8,128)(2,1)S(1)}, bf16[128,2048]{1,0:T(8,128)(2,1)S(1)}, u32[]{:S(2)}, u32[]{:S(2)}) collective-permute-start(bf16[128,2048]{1,0:T(8,128)(2,1)S(1)} %copy-done.123), channel_id=1, source_target_pairs={{0,2},{1,3},{2,4},{3,5},{4,6},{5,7},{6,0},{7,1},{8,10},{9,11},{10,... | collective-permute-start | bytes 1572872 | tf_op jit(solution)/shard_map/ppermute | solution.py:35
  370.7 29.7 %collective-permute-start.37 = (bf16[128,2048]{1,0:T(8,128)(2,1)S(1)}, bf16[128,2048]{1,0:T(8,128)(2,1)S(1)}, u32[]{:S(2)}, u32[]{:S(2)}) collective-permute-start(bf16[128,2048]{1,0:T(8,128)(2,1)S(1)} %copy-done.121), channel_id=1, source_target_pairs={{0,4},{1,5},{2,6},{3,7},{4,0},{5,1},{6,2},{7,3},{8,12},{9,13},{10,... | collective-permute-start | bytes 1572872 | tf_op jit(solution)/shard_map/ppermute | solution.py:35
  377.4 23.0 %collective-permute-start.38 = (bf16[128,2048]{1,0:T(8,128)(2,1)S(1)}, bf16[128,2048]{1,0:T(8,128)(2,1)S(1)}, u32[]{:S(2)}, u32[]{:S(2)}) collective-permute-start(bf16[128,2048]{1,0:T(8,128)(2,1)S(1)} %copy-done.119), channel_id=1, source_target_pairs={{0,6},{1,7},{2,0},{3,1},{4,2},{5,3},{6,4},{7,5},{8,14},{9,15},{10,... | collective-permute-start | bytes 1572872 | tf_op jit(solution)/shard_map/ppermute | solution.py:35
  377.4 22.0 %collective-permute-start.50 = (bf16[192,384]{1,0:T(8,128)(2,1)S(1)}, bf16[192,384]{1,0:T(8,128)(2,1)S(1)}, u32[]{:S(2)}, u32[]{:S(2)}) collective-permute-start(bf16[192,384]{1,0:T(8,128)(2,1)S(1)} %shard_map.200), channel_id=1, source_target_pairs={{0,6},{1,7},{2,0},{3,1},{4,2},{5,3},{6,4},{7,5},{8,14},{9,15},{10,... | collective-permute-start | bytes 442376 | tf_op jit(solution)/shard_map/ppermute | solution.py:35
  400.4 24.6 %collective-permute-start.53 = (bf16[4,192,384]{2,1,0:T(8,128)(2,1)}, bf16[4,192,384]{2,1,0:T(8,128)(2,1)}, u32[]{:S(2)}, u32[]{:S(2)}) collective-permute-start(bf16[4,192,384]{2,1,0:T(8,128)(2,1)} %pad_maximum_fusion.1), channel_id=1, source_target_pairs={{0,1},{1,0},{2,3},{3,2},{4,5},{5,4},{6,7},{7,6},{8,9},{9,8},{10,11... | collective-permute-start | bytes 1769480 | tf_op jit(solution)/shard_map/ppermute | solution.py:39
  402.5 17.9 %collective-permute-start.48 = (bf16[16,2944]{1,0:T(8,128)(2,1)S(1)}, bf16[16,2944]{1,0:T(8,128)(2,1)S(1)}, u32[]{:S(2)}, u32[]{:S(2)}) collective-permute-start(bf16[16,2944]{1,0:T(8,128)(2,1)S(1)} %shard_map.199), channel_id=1, source_target_pairs={{0,2},{1,3},{2,4},{3,5},{4,6},{5,7},{6,0},{7,1},{8,10},{9,11},{10,... | collective-permute-start | bytes 282632 | tf_op jit(solution)/shard_map/ppermute | solution.py:35
  403.7 17.2 %collective-permute-start.47 = (bf16[16,2944]{1,0:T(8,128)(2,1)S(1)}, bf16[16,2944]{1,0:T(8,128)(2,1)S(1)}, u32[]{:S(2)}, u32[]{:S(2)}) collective-permute-start(bf16[16,2944]{1,0:T(8,128)(2,1)S(1)} %shard_map.199), channel_id=1, source_target_pairs={{0,4},{1,5},{2,6},{3,7},{4,0},{5,1},{6,2},{7,3},{8,12},{9,13},{10,... | collective-permute-start | bytes 282632 | tf_op jit(solution)/shard_map/ppermute | solution.py:35
  416.1 27.7 %collective-permute-start.39 = (bf16[128,2176]{1,0:T(8,128)(2,1)}, bf16[128,2176]{1,0:T(8,128)(2,1)}, u32[]{:S(2)}, u32[]{:S(2)}) collective-permute-start(bf16[128,2176]{1,0:T(8,128)(2,1)} %get-tuple-element.148), channel_id=1, source_target_pairs={{0,2},{1,3},{2,4},{3,5},{4,6},{5,7},{6,0},{7,1},{8,10},{9,11},{10,... | collective-permute-start | bytes 1671176 | tf_op jit(solution)/shard_map/ppermute | solution.py:35
  420.3 23.4 %collective-permute-start.40 = (bf16[128,2176]{1,0:T(8,128)(2,1)}, bf16[128,2176]{1,0:T(8,128)(2,1)S(1)}, u32[]{:S(2)}, u32[]{:S(2)}) collective-permute-start(bf16[128,2176]{1,0:T(8,128)(2,1)} %get-tuple-element.149), channel_id=1, source_target_pairs={{0,4},{1,5},{2,6},{3,7},{4,0},{5,1},{6,2},{7,3},{8,12},{9,13},{10,... | collective-permute-start | bytes 1671176 | tf_op jit(solution)/shard_map/ppermute | solution.py:35
  420.9 26.0 %collective-permute-start.41 = (bf16[128,2176]{1,0:T(8,128)(2,1)}, bf16[128,2176]{1,0:T(8,128)(2,1)}, u32[]{:S(2)}, u32[]{:S(2)}) collective-permute-start(bf16[128,2176]{1,0:T(8,128)(2,1)} %get-tuple-element.150), channel_id=1, source_target_pairs={{0,6},{1,7},{2,0},{3,1},{4,2},{5,3},{6,4},{7,5},{8,14},{9,15},{10,... | collective-permute-start | bytes 1671176 | tf_op jit(solution)/shard_map/ppermute | solution.py:35
  424.7 24.6 %collective-permute-start.49 = (bf16[4,16,2944]{2,1,0:T(8,128)(2,1)}, bf16[4,16,2944]{2,1,0:T(8,128)(2,1)}, u32[]{:S(2)}, u32[]{:S(2)}) collective-permute-start(bf16[4,16,2944]{2,1,0:T(8,128)(2,1)} %pad_maximum_fusion.4), channel_id=1, source_target_pairs={{0,1},{1,0},{2,3},{3,2},{4,5},{5,4},{6,7},{7,6},{8,9},{9,8},{10,11... | collective-permute-start | bytes 1130504 | tf_op jit(solution)/shard_map/ppermute | solution.py:39
  (164 other events, 1004.9 us)
Sparse Core Ops, SparseCore 0:
  14.0 33.3 all-gather.7
  49.0 30.8 all-gather.5
  95.2 103.5 all-gather.9
